TPU v7x, 32 devices: a whole 2x2x4 slice. The times are simulated.
32 devices in a mesh: blk: 8 (over z, x), batch: 4 (over y, core).
Axes of the slice: x: 2, y: 2, z: 4, core: 2. Of those that a mesh axis runs over, the one named last changes fastest.
Arguments:
- byte_states: bfloat16 [8, 1024, 512], P('batch', 'blk'), may hold values from -6 to 6
- word_start: int32 [8, 1024], P('batch', 'blk'), may hold values from 0 to 1023, as said below
- bucket_of: int32 [2047], replicated, may hold values from 0 to 31, as said below
- conv_two: bfloat16 [2, 512], replicated, may hold values from -4 to 4
- conv_three: bfloat16 [3, 512], replicated, may hold values from -4 to 4
- conv_four: bfloat16 [4, 512], replicated, may hold values from -4 to 4
- w_join: bfloat16 [512, 512], replicated, may hold values from -0.25 to 0.25
- norm_attn: bfloat16 [512], replicated, may hold values from 0.25 to 1.75
- w_query: bfloat16 [512, 512], replicated, may hold values from -0.0625 to 0.0625
- w_key: bfloat16 [512, 512], replicated, may hold values from -0.25 to 0.25
- w_value: bfloat16 [512, 512], replicated, may hold values from -0.25 to 0.25
- w_out: bfloat16 [512, 512], replicated, may hold values from -1.5 to 1.5
- rel_bias: bfloat16 [32, 8], replicated, may hold values from -4 to 4
- norm_ffn: bfloat16 [512], replicated, may hold values from 0.25 to 1.75
- w_gate: bfloat16 [512, 2048], replicated, may hold values from -0.25 to 0.25
- w_up: bfloat16 [512, 2048], replicated, may hold values from -0.25 to 0.25
- w_down: bfloat16 [2048, 512], replicated, may hold values from -0.125 to 0.125
- grad_output: bfloat16 [8, 1024, 512], P('batch', 'blk'), may hold values from -6 to 6
Outputs:
- output: bfloat16 [8, 1024, 512], P('batch', 'blk')
- grad_states: float32 [8, 1024, 512], P('batch', 'blk')
- grad_conv_two: float32 [2, 512], replicated
- grad_conv_three: float32 [3, 512], replicated
- grad_conv_four: float32 [4, 512], replicated
- grad_w_join: float32 [512, 512], replicated
- grad_norm_attn: float32 [512], replicated
- grad_w_query: float32 [512, 512], replicated
- grad_w_key: float32 [512, 512], replicated
- grad_w_value: float32 [512, 512], replicated
- grad_w_out: float32 [512, 512], replicated
- grad_rel_bias: float32 [32, 8], replicated
- grad_norm_ffn: float32 [512], replicated
- grad_w_gate: float32 [512, 2048], replicated
- grad_w_up: float32 [512, 2048], replicated
- grad_w_down: float32 [2048, 512], replicated
Inputs may be any that keep to these rules, and one draw needn't show every extreme that they name: word_start[b, t] is at most t, equals t or word_start[b, t - 1], and is 0 at t = 0; a word never begins at a byte t > 0 with t % 128 == 0; the last byte of every sequence is a word of its own. bucket_of[r + 1023] is the bucket of a key r places after its query: buckets 0 to 15 for r <= 0, the others for r > 0; on each side the bucket never falls as |r| grows, and each |r| below 8 has a bucket of its own.
All inputs are finite; a program needn't handle non-finite values.
Results may differ from a plain program's by a relative error of at most 0.018.
Values may be sent and summed in bfloat16 or wider, within the bound.
No kernel may reach another device: no remote copies, remote signals or barrier semaphores. Data moves between devices by JAX's collectives and lax.ppermute only.
A program may use at most 128 MiB of HBM per device.

v0:
```python
from functools import partial

import jax
import jax.numpy as jnp
from jax import lax
from jax.sharding import PartitionSpec as P

norm_eps = 1e-06


def for_sending(x):
    return jax.tree.map(lambda a: a.astype(jnp.bfloat16) if a.dtype == jnp.float32 else a, x)


def passed_along(block, axis, distance):
    devices = range(lax.axis_size(axis))
    route = [((i - distance) % len(devices), i) for i in devices]
    return lax.ppermute(block, axis, route)


def shifted(block, axis, distance):
    devices = range(lax.axis_size(axis))
    route = [(i - distance, i) for i in devices if i - distance in devices]
    return lax.ppermute(block, axis, route)


def rms_scale(values, gain_vec):
    return (
        values * lax.rsqrt(jnp.mean(values * values, axis=-1, keepdims=True) + norm_eps) * gain_vec
    )


def gelu_tanh(values):
    return jax.nn.gelu(values, approximate=True)


def project(left_side, right_side):
    return jnp.dot(left_side, right_side, preferred_element_type=jnp.float32)


def project_back(left_side, right_side):
    return lax.dot_general(
        left_side, right_side, (((1,), (1,)), ((), ())), preferred_element_type=jnp.float32
    )


def over_rows(left_side, right_side):
    return lax.dot_general(
        left_side, right_side, (((0,), (0,)), ((), ())), preferred_element_type=jnp.float32
    )


def bias_block(bucket_of, rel_bias, query_pos, key_start, key_count, length):
    key_pos = key_start + jnp.arange(key_count, dtype=jnp.int32)
    buckets = jnp.take(bucket_of, key_pos[None, :] - query_pos[:, None] + length - 1)
    table_size = rel_bias.shape[0]
    onehot = (buckets[:, :, None] == jnp.arange(table_size, dtype=jnp.int32)).astype(jnp.bfloat16)
    pair_bias = jnp.einsum("qkb,bh->hqk", onehot, rel_bias, preferred_element_type=jnp.float32)
    return (pair_bias, onehot)


def split_pair(key_piece, head_count, head_dim):
    sequences, key_count = (key_piece.shape[0], key_piece.shape[1])
    key_heads = key_piece[:, :, 0, :].reshape(sequences, key_count, head_count, head_dim)
    value_heads = key_piece[:, :, 1, :].reshape(sequences, key_count, head_count, head_dim)
    return (key_heads, value_heads)


def fold_keys(running, key_piece, key_start, queries, query_pos, bucket_of, rel_bias, length):
    head_count, head_dim = (queries.shape[2], queries.shape[3])
    key_heads, value_heads = split_pair(key_piece, head_count, head_dim)
    pair_bias, onehot = bias_block(
        bucket_of, rel_bias, query_pos, key_start, key_piece.shape[1], length
    )
    scores = (
        jnp.einsum("sqhd,skhd->shqk", queries, key_heads, preferred_element_type=jnp.float32)
        + pair_bias[None]
    )
    weights = jnp.exp(scores)
    totals = jnp.sum(weights, axis=-1)
    mixed_sum = jnp.einsum(
        "shqk,skhd->sqhd",
        weights.astype(jnp.bfloat16),
        value_heads,
        preferred_element_type=jnp.float32,
    )
    return (totals, mixed_sum)


def key_grads(
    key_piece, key_start, queries, grad_mix, shift_term, query_pos, bucket_of, rel_bias, length
):
    sequences, key_count = (key_piece.shape[0], key_piece.shape[1])
    head_count, head_dim = (queries.shape[2], queries.shape[3])
    key_heads, value_heads = split_pair(key_piece, head_count, head_dim)
    pair_bias, onehot = bias_block(bucket_of, rel_bias, query_pos, key_start, key_count, length)
    scores = (
        jnp.einsum("sqhd,skhd->shqk", queries, key_heads, preferred_element_type=jnp.float32)
        + pair_bias[None]
    )
    weights = jnp.exp(scores)
    grad_value = jnp.einsum(
        "shqk,sqhd->skhd",
        weights.astype(jnp.bfloat16),
        grad_mix,
        preferred_element_type=jnp.float32,
    )
    grad_weight = jnp.einsum(
        "sqhd,skhd->shqk", grad_mix, value_heads, preferred_element_type=jnp.float32
    )
    grad_score = (weights * (grad_weight - shift_term[:, :, :, None])).astype(jnp.bfloat16)
    grad_query = jnp.einsum(
        "shqk,skhd->sqhd", grad_score, key_heads, preferred_element_type=jnp.float32
    )
    grad_key = jnp.einsum(
        "shqk,sqhd->skhd", grad_score, queries, preferred_element_type=jnp.float32
    )
    grad_table = jnp.einsum("shqk,qkb->bh", grad_score, onehot, preferred_element_type=jnp.float32)
    grad_pair = jnp.stack(
        [
            grad_key.reshape(sequences, key_count, head_count * head_dim),
            grad_value.reshape(sequences, key_count, head_count * head_dim),
        ],
        axis=2,
    )
    return (grad_query, grad_pair, grad_table)


def keys_onward(key_piece):
    return jax.tree.map(
        lambda part, own: part.astype(own.dtype),
        passed_along(for_sending(key_piece), "blk", 1),
        key_piece,
    )


def grads_onward(grad_sum):
    return passed_along(grad_sum, "blk", 1)


def per_device(
    byte_states,
    word_start,
    bucket_of,
    conv_two,
    conv_three,
    conv_four,
    w_join,
    norm_attn,
    w_query,
    w_key,
    w_value,
    w_out,
    rel_bias,
    norm_ffn,
    w_gate,
    w_up,
    w_down,
    grad_output,
):
    sequences, block_rows, model_width = byte_states.shape
    blocks = lax.axis_size("blk")
    length = block_rows * blocks
    block_index = lax.axis_index("blk")
    head_count = rel_bias.shape[1]
    head_dim = model_width // head_count
    flat_rows = sequences * block_rows
    positions = block_index * block_rows + jnp.arange(block_rows, dtype=jnp.int32)
    two_f, three_f, four_f = (
        conv_two.astype(jnp.float32),
        conv_three.astype(jnp.float32),
        conv_four.astype(jnp.float32),
    )
    tap_list = [
        two_f[0] + three_f[0] + four_f[0],
        two_f[1] + three_f[1] + four_f[1],
        three_f[2] + four_f[2],
        four_f[3],
    ]
    rim_rows = shifted(byte_states[:, block_rows - 3 :, :], "blk", 1)
    extended = jnp.concatenate([rim_rows, byte_states], axis=1).astype(jnp.float32)
    keep_list = [
        (positions[None, :] - offset >= word_start).astype(jnp.float32)[:, :, None]
        for offset in range(4)
    ]
    ngram_sum = jnp.zeros((sequences, block_rows, model_width), jnp.float32)
    for offset in range(4):
        ngram_sum = (
            ngram_sum
            + tap_list[offset]
            * keep_list[offset]
            * extended[:, 3 - offset : 3 - offset + block_rows, :]
        )
    ngram_low = ngram_sum.reshape(flat_rows, model_width).astype(jnp.bfloat16)
    joined_states = byte_states.reshape(flat_rows, model_width).astype(jnp.float32) + project(
        ngram_low, w_join
    )
    gain_attn = norm_attn.astype(jnp.float32)
    normed_attn = rms_scale(joined_states, gain_attn).astype(jnp.bfloat16)
    queries = (
        project(normed_attn, w_query)
        .astype(jnp.bfloat16)
        .reshape(sequences, block_rows, head_count, head_dim)
    )
    keys_low = (
        project(normed_attn, w_key).astype(jnp.bfloat16).reshape(sequences, block_rows, model_width)
    )
    values_low = (
        project(normed_attn, w_value)
        .astype(jnp.bfloat16)
        .reshape(sequences, block_rows, model_width)
    )
    key_values = jnp.stack([keys_low, values_low], axis=2)
    fold_fn = partial(
        fold_keys,
        queries=queries,
        query_pos=positions,
        bucket_of=bucket_of,
        rel_bias=rel_bias,
        length=length,
    )
    start_totals = jnp.zeros((sequences, head_count, block_rows), jnp.float32)
    start_mix = jnp.zeros((sequences, block_rows, head_count, head_dim), jnp.float32)
    totals, mixed_sum = fold_fn(
        (start_totals, start_mix),
        lax.all_gather(key_values, "blk", axis=1, tiled=True),
        jnp.int32(0),
    )
    total_cols = jnp.transpose(totals, (0, 2, 1))[:, :, :, None]
    attended = mixed_sum / total_cols
    attended_low = attended.reshape(flat_rows, model_width).astype(jnp.bfloat16)
    mid_states = joined_states + project(attended_low, w_out)
    gain_ffn = norm_ffn.astype(jnp.float32)
    normed_ffn = rms_scale(mid_states, gain_ffn).astype(jnp.bfloat16)
    gate_proj = project(normed_ffn, w_gate)
    up_proj = project(normed_ffn, w_up)
    gelu_gate, gelu_pull = jax.vjp(gelu_tanh, gate_proj)
    hidden = (gelu_gate * up_proj).astype(jnp.bfloat16)
    output = (
        (mid_states + project(hidden, w_down))
        .astype(jnp.bfloat16)
        .reshape(sequences, block_rows, model_width)
    )
    grad_low = grad_output.reshape(flat_rows, model_width)
    grad_w_down = over_rows(hidden, grad_low)
    grad_hidden = project_back(grad_low, w_down)
    grad_gate = gelu_pull(grad_hidden * up_proj)[0].astype(jnp.bfloat16)
    grad_up = (grad_hidden * gelu_gate).astype(jnp.bfloat16)
    grad_w_gate = over_rows(normed_ffn, grad_gate)
    grad_w_up = over_rows(normed_ffn, grad_up)
    grad_normed_ffn = project_back(grad_gate, w_gate) + project_back(grad_up, w_up)
    grad_mid_norm, grad_norm_ffn = jax.vjp(rms_scale, mid_states, gain_ffn)[1](grad_normed_ffn)
    grad_mid = grad_low.astype(jnp.float32) + grad_mid_norm
    grad_mid_low = grad_mid.astype(jnp.bfloat16)
    grad_w_out = over_rows(attended_low, grad_mid_low)
    grad_attended = project_back(grad_mid_low, w_out).reshape(
        sequences, block_rows, head_count, head_dim
    )
    grad_mix = (grad_attended / total_cols).astype(jnp.bfloat16)
    shift_term = jnp.transpose(jnp.sum(grad_attended * attended, axis=-1), (0, 2, 1)) / totals
    grads_fn = partial(
        key_grads,
        queries=queries,
        grad_mix=grad_mix,
        shift_term=shift_term,
        query_pos=positions,
        bucket_of=bucket_of,
        rel_bias=rel_bias,
        length=length,
    )
    lane_list = [(keys_onward, grads_onward, 1, 0)]
    pieces = (key_values,)
    pair_sums = tuple((jnp.zeros(key_piece.shape, jnp.float32) for key_piece in pieces))

    def visit_block(step_index, cycle_state):
        held, held_sums, grad_query, grad_table = cycle_state
        new_sums = []
        for lane_spec, key_piece, grad_sum in zip(lane_list, held, held_sums):
            owner_index = (block_index - lane_spec[2] * step_index) % blocks
            query_add, pair_add, table_add = grads_fn(
                key_piece, owner_index * block_rows + lane_spec[3]
            )
            grad_query = grad_query + query_add
            grad_table = grad_table + table_add
            new_sums.append(grad_sum + pair_add)
        return (held, tuple(new_sums), grad_query, grad_table)

    def travel(step_index, cycle_state):
        held, held_sums, grad_query, grad_table = visit_block(step_index, cycle_state)
        held = tuple((lane_spec[0](key_piece) for lane_spec, key_piece in zip(lane_list, held)))
        held_sums = tuple(
            (lane_spec[1](grad_sum) for lane_spec, grad_sum in zip(lane_list, held_sums))
        )
        return (held, held_sums, grad_query, grad_table)

    cycle_state = (
        pieces,
        pair_sums,
        jnp.zeros((sequences, block_rows, head_count, head_dim), jnp.float32),
        jnp.zeros(rel_bias.shape, jnp.float32),
    )
    cycle_state = lax.fori_loop(0, blocks - 1, travel, cycle_state)
    pieces, pair_sums, grad_query, grad_rel_bias = visit_block(blocks - 1, cycle_state)
    pair_sums = tuple((lane_spec[1](grad_sum) for lane_spec, grad_sum in zip(lane_list, pair_sums)))
    grad_pairs = jnp.concatenate(pair_sums, axis=1)
    grad_query_low = grad_query.reshape(flat_rows, model_width).astype(jnp.bfloat16)
    grad_key_low = grad_pairs[:, :, 0, :].reshape(flat_rows, model_width).astype(jnp.bfloat16)
    grad_value_low = grad_pairs[:, :, 1, :].reshape(flat_rows, model_width).astype(jnp.bfloat16)
    grad_w_query = over_rows(normed_attn, grad_query_low)
    grad_w_key = over_rows(normed_attn, grad_key_low)
    grad_w_value = over_rows(normed_attn, grad_value_low)
    grad_normed_attn = (
        project_back(grad_query_low, w_query)
        + project_back(grad_key_low, w_key)
        + project_back(grad_value_low, w_value)
    )
    grad_joined_norm, grad_norm_attn = jax.vjp(rms_scale, joined_states, gain_attn)[1](
        grad_normed_attn
    )
    grad_joined = grad_mid + grad_joined_norm
    grad_joined_low = grad_joined.astype(jnp.bfloat16)
    grad_w_join = over_rows(ngram_low, grad_joined_low)
    grad_ngram = project_back(grad_joined_low, w_join).reshape(sequences, block_rows, model_width)
    grad_taps = []
    grad_extended = jnp.zeros((sequences, block_rows + 3, model_width), jnp.float32)
    for offset in range(4):
        masked = keep_list[offset] * grad_ngram
        grad_taps.append(
            jnp.sum(masked * extended[:, 3 - offset : 3 - offset + block_rows, :], axis=(0, 1))
        )
        grad_extended = grad_extended.at[:, 3 - offset : 3 - offset + block_rows, :].add(
            tap_list[offset] * masked
        )
    spill_rows = shifted(grad_extended[:, :3, :], "blk", -1)
    grad_states = grad_joined.reshape(sequences, block_rows, model_width) + grad_extended[:, 3:, :]
    grad_states = grad_states.at[:, block_rows - 3 :, :].add(spill_rows)
    grad_conv_two = jnp.stack(grad_taps[:2])
    grad_conv_three = jnp.stack(grad_taps[:3])
    grad_conv_four = jnp.stack(grad_taps)
    summed = lax.psum(
        (
            grad_conv_two,
            grad_conv_three,
            grad_conv_four,
            grad_w_join,
            grad_norm_attn,
            grad_w_query,
            grad_w_key,
            grad_w_value,
            grad_w_out,
            grad_rel_bias,
            grad_norm_ffn,
            grad_w_gate,
            grad_w_up,
            grad_w_down,
        ),
        ("blk", "batch"),
    )
    return (
        output,
        grad_states,
        summed[0],
        summed[1],
        summed[2],
        summed[3],
        summed[4],
        summed[5],
        summed[6],
        summed[7],
        summed[8],
        summed[9],
        summed[10],
        summed[11],
        summed[12],
        summed[13],
    )


def solution(mesh):
    return jax.shard_map(
        per_device,
        mesh=mesh,
        in_specs=(
            P("batch", "blk", None),
            P("batch", "blk"),
            P(),
            P(),
            P(),
            P(),
            P(),
            P(),
            P(),
            P(),
            P(),
            P(),
            P(),
            P(),
            P(),
            P(),
            P(),
            P("batch", "blk", None),
        ),
        out_specs=(
            P("batch", "blk", None),
            P("batch", "blk", None),
            P(),
            P(),
            P(),
            P(),
            P(),
            P(),
            P(),
            P(),
            P(),
            P(),
            P(),
            P(),
            P(),
            P(),
        ),
        check_vma=False,
    )
```

profile of v0, /device:TPU:0, one launch (start us, length us, event | category | flops | bytes accessed | tf_op | source)
XLA Modules:
  0.0 2209.1 jit_solution(13811807753383481062)
XLA Ops:
  8.1 4.8 collective-permute-start.2
  22.3 90.5 %gather_fusion.2 = s32[16384]{0:T(1024)S(1)} fusion(s32[2047]{0:T(1024)S(1)} %copy-done.1, s32[16384]{0:T(1024)S(1)} %fusion.73), kind=kCustom, calls=%fused_computation.1.clone | custom fusion | bytes 196608 | tf_op jit(solution)/shard_map/jit(_take)/gather | solution.py:55
  117.4 725.0 %gather_fusion.1 = s32[131072]{0:T(1024)S(1)} fusion(s32[2047]{0:T(1024)S(1)} %copy-done.1, s32[131072]{0:T(1024)S(1)} %broadcast_clamp_fusion), kind=kCustom, calls=%fused_computation.2 | custom fusion | bytes 1572864 | tf_op jit(solution)/shard_map/jit(_take)/gather | solution.py:55
  845.7 4.4 copy.75
  880.4 977.1 %while.29 = (s32[]{:T(128)}, bf16[2,128,2,512]{1,3,0,2:T(8,128)(2,1)}, f32[2,128,2,512]{1,3,0,2:T(8,128)}, f32[2,128,8,64]{1,3,2,0:T(8,128)}, f32[32,8]{0,1:T(8,...) while((s32[]{:T(128)}, ...), condition=%wide.region_7.9_spmd.clone, body=%wide.region_5.0_spmd.clone.sunk | while | flops 188334864 | bytes 26097536 | solution.py:302
  880.5 90.5 %gather_fusion = s32[16384]{0:T(1024)S(1)} fusion(s32[2047]{0:T(1024)S(1)} %get-tuple-element.746, s32[16384]{0:T(1024)S(1)} %fusion.193), kind=kCustom, calls=%fused_computation.clone.clone.1 | custom fusion | bytes 196608 | tf_op jit(solution)/shard_map/while/body/eval_jaxpr/jit(_take)/gather | solution.py:55
  991.4 31.3 %collective-permute-done = bf16[2,128,2,512]{1,3,0,2:T(8,128)(2,1)} collective-permute-done((bf16[2,128,2,512]{1,3,0,2:T(8,128)(2,1)S(1)}, bf16[2,128,2,512]{1,3,0,2:T(8,128)(2,1)}, u32[]{:S(2)}, u32[]{:S(2)}) %collective-permute-start) | collective-permute-done | bytes 524320 | tf_op jit(solution)/shard_map/while/body/eval_jaxpr/ppermute | solution.py:18
  1022.8 90.5 %gather_fusion = s32[16384]{0:T(1024)S(1)} fusion(s32[2047]{0:T(1024)S(1)} %get-tuple-element.746, s32[16384]{0:T(1024)S(1)} %fusion.193), kind=kCustom, calls=%fused_computation.clone.clone.1 | custom fusion | bytes 196608 | tf_op jit(solution)/shard_map/while/body/eval_jaxpr/jit(_take)/gather | solution.py:55
  1132.9 31.2 %collective-permute-done = bf16[2,128,2,512]{1,3,0,2:T(8,128)(2,1)} collective-permute-done((bf16[2,128,2,512]{1,3,0,2:T(8,128)(2,1)S(1)}, bf16[2,128,2,512]{1,3,0,2:T(8,128)(2,1)}, u32[]{:S(2)}, u32[]{:S(2)}) %collective-permute-start) | collective-permute-done | bytes 524320 | tf_op jit(solution)/shard_map/while/body/eval_jaxpr/ppermute | solution.py:18
  1164.2 90.5 %gather_fusion = s32[16384]{0:T(1024)S(1)} fusion(s32[2047]{0:T(1024)S(1)} %get-tuple-element.746, s32[16384]{0:T(1024)S(1)} %fusion.193), kind=kCustom, calls=%fused_computation.clone.clone.1 | custom fusion | bytes 196608 | tf_op jit(solution)/shard_map/while/body/eval_jaxpr/jit(_take)/gather | solution.py:55
  1273.1 31.5 %collective-permute-done = bf16[2,128,2,512]{1,3,0,2:T(8,128)(2,1)} collective-permute-done((bf16[2,128,2,512]{1,3,0,2:T(8,128)(2,1)S(1)}, bf16[2,128,2,512]{1,3,0,2:T(8,128)(2,1)}, u32[]{:S(2)}, u32[]{:S(2)}) %collective-permute-start) | collective-permute-done | bytes 524320 | tf_op jit(solution)/shard_map/while/body/eval_jaxpr/ppermute | solution.py:18
  1304.7 90.5 %gather_fusion = s32[16384]{0:T(1024)S(1)} fusion(s32[2047]{0:T(1024)S(1)} %get-tuple-element.746, s32[16384]{0:T(1024)S(1)} %fusion.193), kind=kCustom, calls=%fused_computation.clone.clone.1 | custom fusion | bytes 196608 | tf_op jit(solution)/shard_map/while/body/eval_jaxpr/jit(_take)/gather | solution.py:55
  1413.6 30.6 %collective-permute-done = bf16[2,128,2,512]{1,3,0,2:T(8,128)(2,1)} collective-permute-done((bf16[2,128,2,512]{1,3,0,2:T(8,128)(2,1)S(1)}, bf16[2,128,2,512]{1,3,0,2:T(8,128)(2,1)}, u32[]{:S(2)}, u32[]{:S(2)}) %collective-permute-start) | collective-permute-done | bytes 524320 | tf_op jit(solution)/shard_map/while/body/eval_jaxpr/ppermute | solution.py:18
  1444.2 90.5 %gather_fusion = s32[16384]{0:T(1024)S(1)} fusion(s32[2047]{0:T(1024)S(1)} %get-tuple-element.746, s32[16384]{0:T(1024)S(1)} %fusion.193), kind=kCustom, calls=%fused_computation.clone.clone.1 | custom fusion | bytes 196608 | tf_op jit(solution)/shard_map/while/body/eval_jaxpr/jit(_take)/gather | solution.py:55
  1553.1 29.6 %collective-permute-done = bf16[2,128,2,512]{1,3,0,2:T(8,128)(2,1)} collective-permute-done((bf16[2,128,2,512]{1,3,0,2:T(8,128)(2,1)S(1)}, bf16[2,128,2,512]{1,3,0,2:T(8,128)(2,1)}, u32[]{:S(2)}, u32[]{:S(2)}) %collective-permute-start) | collective-permute-done | bytes 524320 | tf_op jit(solution)/shard_map/while/body/eval_jaxpr/ppermute | solution.py:18
  1582.9 90.5 %gather_fusion = s32[16384]{0:T(1024)S(1)} fusion(s32[2047]{0:T(1024)S(1)} %get-tuple-element.746, s32[16384]{0:T(1024)S(1)} %fusion.193), kind=kCustom, calls=%fused_computation.clone.clone.1 | custom fusion | bytes 196608 | tf_op jit(solution)/shard_map/while/body/eval_jaxpr/jit(_take)/gather | solution.py:55
  1691.8 28.7 %collective-permute-done = bf16[2,128,2,512]{1,3,0,2:T(8,128)(2,1)} collective-permute-done((bf16[2,128,2,512]{1,3,0,2:T(8,128)(2,1)S(1)}, bf16[2,128,2,512]{1,3,0,2:T(8,128)(2,1)}, u32[]{:S(2)}, u32[]{:S(2)}) %collective-permute-start) | collective-permute-done | bytes 524320 | tf_op jit(solution)/shard_map/while/body/eval_jaxpr/ppermute | solution.py:18
  1720.6 90.5 %gather_fusion = s32[16384]{0:T(1024)S(1)} fusion(s32[2047]{0:T(1024)S(1)} %get-tuple-element.746, s32[16384]{0:T(1024)S(1)} %fusion.193), kind=kCustom, calls=%fused_computation.clone.clone.1 | custom fusion | bytes 196608 | tf_op jit(solution)/shard_map/while/body/eval_jaxpr/jit(_take)/gather | solution.py:55
  1829.5 27.8 %collective-permute-done = bf16[2,128,2,512]{1,3,0,2:T(8,128)(2,1)} collective-permute-done((bf16[2,128,2,512]{1,3,0,2:T(8,128)(2,1)S(1)}, bf16[2,128,2,512]{1,3,0,2:T(8,128)(2,1)}, u32[]{:S(2)}, u32[]{:S(2)}) %collective-permute-start) | collective-permute-done | bytes 524320 | tf_op jit(solution)/shard_map/while/body/eval_jaxpr/ppermute | solution.py:18
  1877.1 8.7 collective-permute-done.3
  1900.1 3.3 scatter-add.19
  1905.3 3.3 scatter-add.20
  1913.2 41.1 %all-reduce.1 = (f32[2,512]{1,0:T(2,128)}, f32[3,512]{1,0:T(4,128)}, f32[4,512]{1,0:T(4,128)}, f32[512]{0:T(512)}, f32[32,8]{0,1:T(8,128)}, /*index=5*/f32[512]{0:T(512)}) all-reduce(f32[2,512]{1,0:T(2,128)S(1)} %pad_maximum_fusion.3, f32[3,512]{1,0:T(4,128)S(1)} %pad_maximum_fusion.1, ...), channel_id=1, replica_groups=mesh['blk'=8,'batch'=4] {'blk','batch'}, use_global_device_ids=true, to_apply=%region_11.13 | all-reduce | flops 5888 | bytes 47104 | tf_op jit(solution)/shard_map/psum | solution.py:340
  1954.5 231.3 %all-reduce.5.cloned.1.call-done = (f32[512,512]{1,0:T(8,128)}, f32[512,512]{1,0:T(8,128)}, f32[512,512]{1,0:T(8,128)}, f32[512,512]{1,0:T(8,128)}, f32[512,512]...) async-done(((f32[512,512]{1,0:T(8,128)}, f32[512,512]{1,0:T(8,128)}, f32[512,512]{1,0:T(8,128)}, f32[512,512]{1,0:T(8,128)}, ...) | async-done | bytes 17825808 | tf_op jit(solution)/shard_map/psum | solution.py:340
  (423 shorter events, 235.6 us)
Async XLA Ops:
  7.2 856.3 %copy-start = (bf16[2048,512]{1,0:T(8,128)(2,1)S(1)}, bf16[2048,512]{1,0:T(8,128)(2,1)}, u32[]{:S(2)}) copy-start(bf16[2048,512]{1,0:T(8,128)(2,1)} %param.48) | copy-start | bytes 6291460
  7.2 844.6 %all-gather.2.cloned.1.call-start = ((), (), s32[]{:S(2)}) async-start(), calls=%async_computation | async-start | bytes 4718592 | tf_op jit(solution)/shard_map/all_gather | solution.py:226
  8.1 9.1 collective-permute-start.2
  13.0 104.1 %copy-start.67 = (s32[128]{0:T(128)}, s32[128]{0:T(128)S(1)}, u32[]{:S(2)}) copy-start(s32[128]{0:T(128)S(1)} %get-tuple-element.620) | copy-start | bytes 1540
  21.5 2164.3 %all-reduce.5.cloned.1.call-start = ((), (), s32[]{:S(2)}) async-start(), calls=%async_computation.1 | async-start | bytes 35651584 | tf_op jit(solution)/shard_map/psum | solution.py:340
  22.3 93.5 %copy-start.46 = (bf16[32,8]{0,1:T(8,128)(2,1)S(1)}, bf16[32,8]{0,1:T(8,128)(2,1)}, u32[]{:S(2)}) copy-start(bf16[32,8]{0,1:T(8,128)(2,1)} %param.44) | copy-start | bytes 1540
  117.4 725.2 %copy-start.68 = (s32[128]{0:T(128)S(1)}, s32[128]{0:T(128)}, u32[]{:S(2)}) copy-start(s32[128]{0:T(128)} %copy-done.67) | copy-start | bytes 1540
  983.8 38.9 %collective-permute-start.1 = (f32[2,128,2,512]{1,3,0,2:T(8,128)}, f32[2,128,2,512]{1,3,0,2:T(8,128)}, u32[]{:S(2)}, u32[]{:S(2)}) collective-permute-start(f32[2,128,2,512]{1,3,0,2:T(8,128)} %maximum_add_fusion.3), channel_id=1, source_target_pairs={{28,0},{0,4},{4,8},{8,12},{12,16},{16,20},{20,24},{24,28},{29,1},{... | collective-permute-start | bytes 3145736 | tf_op jit(solution)/shard_map/while/body/eval_jaxpr/ppermute | solution.py:18
  985.4 37.3 %collective-permute-start = (bf16[2,128,2,512]{1,3,0,2:T(8,128)(2,1)S(1)}, bf16[2,128,2,512]{1,3,0,2:T(8,128)(2,1)}, u32[]{:S(2)}, u32[]{:S(2)}) collective-permute-start(bf16[2,128,2,512]{1,3,0,2:T(8,128)(2,1)S(1)} %copy.131), channel_id=1, source_target_pairs={{28,0},{0,4},{4,8},{8,12},{12,16},{16,20},{20,24},{24,28},{29,1},{... | collective-permute-start | bytes 1572872 | tf_op jit(solution)/shard_map/while/body/eval_jaxpr/ppermute | solution.py:18
  1126.1 37.9 %collective-permute-start.1 = (f32[2,128,2,512]{1,3,0,2:T(8,128)}, f32[2,128,2,512]{1,3,0,2:T(8,128)}, u32[]{:S(2)}, u32[]{:S(2)}) collective-permute-start(f32[2,128,2,512]{1,3,0,2:T(8,128)} %maximum_add_fusion.3), channel_id=1, source_target_pairs={{28,0},{0,4},{4,8},{8,12},{12,16},{16,20},{20,24},{24,28},{29,1},{... | collective-permute-start | bytes 3145736 | tf_op jit(solution)/shard_map/while/body/eval_jaxpr/ppermute | solution.py:18
  1126.2 37.9 %collective-permute-start = (bf16[2,128,2,512]{1,3,0,2:T(8,128)(2,1)S(1)}, bf16[2,128,2,512]{1,3,0,2:T(8,128)(2,1)}, u32[]{:S(2)}, u32[]{:S(2)}) collective-permute-start(bf16[2,128,2,512]{1,3,0,2:T(8,128)(2,1)S(1)} %copy.131), channel_id=1, source_target_pairs={{28,0},{0,4},{4,8},{8,12},{12,16},{16,20},{20,24},{24,28},{29,1},{... | collective-permute-start | bytes 1572872 | tf_op jit(solution)/shard_map/while/body/eval_jaxpr/ppermute | solution.py:18
  1267.5 37.0 %collective-permute-start.1 = (f32[2,128,2,512]{1,3,0,2:T(8,128)}, f32[2,128,2,512]{1,3,0,2:T(8,128)}, u32[]{:S(2)}, u32[]{:S(2)}) collective-permute-start(f32[2,128,2,512]{1,3,0,2:T(8,128)} %maximum_add_fusion.3), channel_id=1, source_target_pairs={{28,0},{0,4},{4,8},{8,12},{12,16},{16,20},{20,24},{24,28},{29,1},{... | collective-permute-start | bytes 3145736 | tf_op jit(solution)/shard_map/while/body/eval_jaxpr/ppermute | solution.py:18
  1267.6 37.0 %collective-permute-start = (bf16[2,128,2,512]{1,3,0,2:T(8,128)(2,1)S(1)}, bf16[2,128,2,512]{1,3,0,2:T(8,128)(2,1)}, u32[]{:S(2)}, u32[]{:S(2)}) collective-permute-start(bf16[2,128,2,512]{1,3,0,2:T(8,128)(2,1)S(1)} %copy.131), channel_id=1, source_target_pairs={{28,0},{0,4},{4,8},{8,12},{12,16},{16,20},{20,24},{24,28},{29,1},{... | collective-permute-start | bytes 1572872 | tf_op jit(solution)/shard_map/while/body/eval_jaxpr/ppermute | solution.py:18
  1408.0 36.1 %collective-permute-start.1 = (f32[2,128,2,512]{1,3,0,2:T(8,128)}, f32[2,128,2,512]{1,3,0,2:T(8,128)}, u32[]{:S(2)}, u32[]{:S(2)}) collective-permute-start(f32[2,128,2,512]{1,3,0,2:T(8,128)} %maximum_add_fusion.3), channel_id=1, source_target_pairs={{28,0},{0,4},{4,8},{8,12},{12,16},{16,20},{20,24},{24,28},{29,1},{... | collective-permute-start | bytes 3145736 | tf_op jit(solution)/shard_map/while/body/eval_jaxpr/ppermute | solution.py:18
  1408.0 36.1 %collective-permute-start = (bf16[2,128,2,512]{1,3,0,2:T(8,128)(2,1)S(1)}, bf16[2,128,2,512]{1,3,0,2:T(8,128)(2,1)}, u32[]{:S(2)}, u32[]{:S(2)}) collective-permute-start(bf16[2,128,2,512]{1,3,0,2:T(8,128)(2,1)S(1)} %copy.131), channel_id=1, source_target_pairs={{28,0},{0,4},{4,8},{8,12},{12,16},{16,20},{20,24},{24,28},{29,1},{... | collective-permute-start | bytes 1572872 | tf_op jit(solution)/shard_map/while/body/eval_jaxpr/ppermute | solution.py:18
  1547.6 35.2 %collective-permute-start.1 = (f32[2,128,2,512]{1,3,0,2:T(8,128)}, f32[2,128,2,512]{1,3,0,2:T(8,128)}, u32[]{:S(2)}, u32[]{:S(2)}) collective-permute-start(f32[2,128,2,512]{1,3,0,2:T(8,128)} %maximum_add_fusion.3), channel_id=1, source_target_pairs={{28,0},{0,4},{4,8},{8,12},{12,16},{16,20},{20,24},{24,28},{29,1},{... | collective-permute-start | bytes 3145736 | tf_op jit(solution)/shard_map/while/body/eval_jaxpr/ppermute | solution.py:18
  1547.6 35.2 %collective-permute-start = (bf16[2,128,2,512]{1,3,0,2:T(8,128)(2,1)S(1)}, bf16[2,128,2,512]{1,3,0,2:T(8,128)(2,1)}, u32[]{:S(2)}, u32[]{:S(2)}) collective-permute-start(bf16[2,128,2,512]{1,3,0,2:T(8,128)(2,1)S(1)} %copy.131), channel_id=1, source_target_pairs={{28,0},{0,4},{4,8},{8,12},{12,16},{16,20},{20,24},{24,28},{29,1},{... | collective-permute-start | bytes 1572872 | tf_op jit(solution)/shard_map/while/body/eval_jaxpr/ppermute | solution.py:18
  1686.2 34.3 %collective-permute-start.1 = (f32[2,128,2,512]{1,3,0,2:T(8,128)}, f32[2,128,2,512]{1,3,0,2:T(8,128)}, u32[]{:S(2)}, u32[]{:S(2)}) collective-permute-start(f32[2,128,2,512]{1,3,0,2:T(8,128)} %maximum_add_fusion.3), channel_id=1, source_target_pairs={{28,0},{0,4},{4,8},{8,12},{12,16},{16,20},{20,24},{24,28},{29,1},{... | collective-permute-start | bytes 3145736 | tf_op jit(solution)/shard_map/while/body/eval_jaxpr/ppermute | solution.py:18
  1686.2 34.3 %collective-permute-start = (bf16[2,128,2,512]{1,3,0,2:T(8,128)(2,1)S(1)}, bf16[2,128,2,512]{1,3,0,2:T(8,128)(2,1)}, u32[]{:S(2)}, u32[]{:S(2)}) collective-permute-start(bf16[2,128,2,512]{1,3,0,2:T(8,128)(2,1)S(1)} %copy.131), channel_id=1, source_target_pairs={{28,0},{0,4},{4,8},{8,12},{12,16},{16,20},{20,24},{24,28},{29,1},{... | collective-permute-start | bytes 1572872 | tf_op jit(solution)/shard_map/while/body/eval_jaxpr/ppermute | solution.py:18
  1823.9 33.3 %collective-permute-start.1 = (f32[2,128,2,512]{1,3,0,2:T(8,128)}, f32[2,128,2,512]{1,3,0,2:T(8,128)}, u32[]{:S(2)}, u32[]{:S(2)}) collective-permute-start(f32[2,128,2,512]{1,3,0,2:T(8,128)} %maximum_add_fusion.3), channel_id=1, source_target_pairs={{28,0},{0,4},{4,8},{8,12},{12,16},{16,20},{20,24},{24,28},{29,1},{... | collective-permute-start | bytes 3145736 | tf_op jit(solution)/shard_map/while/body/eval_jaxpr/ppermute | solution.py:18
  1823.9 33.3 %collective-permute-start = (bf16[2,128,2,512]{1,3,0,2:T(8,128)(2,1)S(1)}, bf16[2,128,2,512]{1,3,0,2:T(8,128)(2,1)}, u32[]{:S(2)}, u32[]{:S(2)}) collective-permute-start(bf16[2,128,2,512]{1,3,0,2:T(8,128)(2,1)S(1)} %copy.131), channel_id=1, source_target_pairs={{28,0},{0,4},{4,8},{8,12},{12,16},{16,20},{20,24},{24,28},{29,1},{... | collective-permute-start | bytes 1572872 | tf_op jit(solution)/shard_map/while/body/eval_jaxpr/ppermute | solution.py:18
  1873.8 11.9 collective-permute-start.3
  1910.6 43.7 %collective-permute-start.4 = (f32[2,3,512]{2,1,0:T(4,128)S(1)}, f32[2,3,512]{2,1,0:T(4,128)S(1)}, u32[]{:S(2)}, u32[]{:S(2)}) collective-permute-start(f32[2,3,512]{2,1,0:T(4,128)S(1)} %slice.271), channel_id=1, source_target_pairs={{4,0},{8,4},{12,8},{16,12},{20,16},{24,20},{28,24},{5,1},{9,5},{13... | collective-permute-start | bytes 36872 | tf_op jit(solution)/shard_map/ppermute | solution.py:24
  1954.5 234.7 %copy-start.43 = (f32[2,128,512]{2,1,0:T(8,128)}, f32[2,128,512]{2,1,0:T(8,128)S(1)}, u32[]{:S(2)}) copy-start(f32[2,128,512]{2,1,0:T(8,128)S(1)} %scatter-add.24) | copy-start | bytes 1572868
  (71 other events, 216.0 us)
Sparse Core Ops, SparseCore 0:
  21.6 75.3 all-gather.1
  1891.2 294.5 all-reduce.4
where the time goes:
time: 2220 us; the launch traced here: 2210 us
  local copies, waits for them, and re-layouts  1540 us (69%)
  waiting for transfers between devices  451 us (20%)
  matrix products  113 us (5%)
  blocking collectives  41.1 us (2%)
  other arithmetic  37.2 us (2%)
    gather x10, local copies, waits for them, and re-layouts, bias_block(): jnp.take(bucket_of, key_pos[None, :] - query_pos[:, None] + length - 1)  1450 us
    psum x1, waiting for transfers between devices, per_device(): lax.psum((grad_conv_two, grad_conv_three, grad_conv_four, grad_w_join, gr...  231 us
    ppermute x15, waiting for transfers between devices, passed_along(): return lax.ppermute(block, axis, route)  219 us
  transfers between devices with their start and end apart: 19, of which 9 were waited for; matrix products, arithmetic and copies ran while one was open for 40% of the time, Pallas kernels for 0%

commit v1 on v0

v1 whole, which is shorter than its diff:
```python
from functools import partial

import jax
import jax.numpy as jnp
from jax import lax
from jax.experimental import pallas as pl
from jax.experimental.pallas import tpu as pltpu
from jax.sharding import PartitionSpec as P

norm_eps = 1e-06
LANES = 128
EDGE = 3
CHUNKS = 4
KEY_BLOCKS = 4
VMEM_LIMIT = 65400 * 1024
GELU_SCALE = 0.7978845608028654
GELU_CUBE = 0.044715


def lasting(micros):
    return pl.CostEstimate(flops=0, transcendentals=0, bytes_accessed=int(micros * 3.5e6))


IN_HBM = pl.BlockSpec(memory_space=pltpu.HBM)


def shifted(block, axis, distance):
    devices = range(lax.axis_size(axis))
    route = [(i - distance, i) for i in devices if i - distance in devices]
    return lax.ppermute(block, axis, route)


def project(left_side, right_side):
    return jnp.dot(left_side, right_side, preferred_element_type=jnp.float32)


def project_back(left_side, right_side):
    return lax.dot_general(
        left_side, right_side, (((1,), (1,)), ((), ())), preferred_element_type=jnp.float32
    )


def over_rows(left_side, right_side):
    return lax.dot_general(
        left_side, right_side, (((0,), (0,)), ((), ())), preferred_element_type=jnp.float32
    )


def turned(low_block):
    return jnp.transpose(low_block.astype(jnp.float32)).astype(jnp.bfloat16)


def inverse_rms(values):
    return lax.rsqrt(jnp.mean(values * values, axis=-1, keepdims=True) + norm_eps)


def rms_back(values, gain, grad):
    scale = inverse_rms(values)
    scaled = values * scale
    gained = gain * grad
    lean = jnp.mean(scaled * gained, axis=-1, keepdims=True)
    return scale * (gained - scaled * lean), jnp.sum(grad * scaled, axis=0, keepdims=True)


def tap_rows(two_ref, three_ref, four_ref):
    two, three, four = (r[...].astype(jnp.float32) for r in (two_ref, three_ref, four_ref))
    return [
        two[0:1] + three[0:1] + four[0:1],
        two[1:2] + three[1:2] + four[1:2],
        three[2:3] + four[2:3],
        four[3:4],
    ]


def keep_columns(start_ref, sequence, first, rows, width):
    starts = jnp.transpose(
        jnp.broadcast_to(start_ref[sequence : sequence + 1, :].astype(jnp.float32), (rows, rows))
    )
    spots = (lax.broadcasted_iota(jnp.int32, (rows, rows), 0) + first).astype(jnp.float32)
    lead = spots - starts
    return [
        jnp.concatenate([(lead >= float(j)).astype(jnp.float32)] * (width // rows), axis=1)
        for j in range(4)
    ]


def front_kernel(*refs, sequences, rows, heads, dim, count):
    width = heads * dim
    given, made, held = refs[:count], refs[count : count + 4], refs[count + 4 : 2 * count + 4]
    joined_ref, normed_ref, ngram_ref, sent_ref, ext_ref, sems = refs[2 * count + 4 :]
    waiting = copies_between(given, held, sems)
    (states_ref, rim_ref, start_ref, two_ref, three_ref, four_ref, wjoin_ref, gain_ref, wq_ref, wk_ref,
     wv_ref) = held
    for copy in waiting[:6]:
        copy.wait()
    taps = tap_rows(two_ref, three_ref, four_ref)
    for s in range(sequences):
        span = slice(s * rows, (s + 1) * rows)
        states = states_ref[s].astype(jnp.float32)
        ext_ref[8 - EDGE : 8, :] = rim_ref[s].astype(jnp.float32)
        ext_ref[8 : 8 + rows, :] = states
        keeps = keep_columns(start_ref, s, lax.axis_index("blk") * rows, rows, width)
        ngram = taps[0] * keeps[0] * states
        for j in range(1, 4):
            ngram = ngram + taps[j] * keeps[j] * ext_ref[8 - j : 8 - j + rows, :]
        low = ngram.astype(jnp.bfloat16)
        ngram_ref[span, :] = low
        if s == 0:
            waiting[6].wait()
        joined_ref[span, :] = states + project(low, wjoin_ref[...])
    done = copies_between((joined_ref, ngram_ref), (made[0], made[2]), sems, count)
    waiting[7].wait()
    joined = joined_ref[...]
    gain = gain_ref[...].astype(jnp.float32).reshape(1, -1)
    normed = (joined * inverse_rms(joined) * gain).astype(jnp.bfloat16)
    normed_ref[...] = normed
    done += copies_between((normed_ref,), (made[1],), sems, count + 2)
    for part, w_ref in enumerate((wq_ref, wk_ref, wv_ref)):
        waiting[8 + part].wait()
        flipped = jnp.transpose(project(normed, w_ref[...])).astype(jnp.bfloat16)
        features = pl.ds(part * dim, dim)
        for h in range(heads):
            for s in range(sequences):
                unit = h * sequences + s
                per_block = sent_ref.shape[1]
                sent_ref[unit // per_block, unit % per_block, part * dim : (part + 1) * dim, :] = flipped[
                    h * dim : (h + 1) * dim, s * rows : (s + 1) * rows
                ]
        done += copies_between(
            (sent_ref.at[:, :, features, :],), (made[3].at[:, :, features, :],), sems, count + 3 + part
        )
    for copy in done:
        copy.wait()


def whole(shape):
    return pl.BlockSpec(shape, lambda *_: (0,) * len(shape))


def front(states, rim, starts, two, three, four, w_join, gain, w_query, w_key, w_value, heads, blocks):
    sequences, rows, width = states.shape
    dim = width // heads
    flat = sequences * rows
    operands = (states, rim, starts, two, three, four, w_join, gain, w_query, w_key, w_value)
    outs = [
        jax.ShapeDtypeStruct((flat, width), jnp.float32),
        jax.ShapeDtypeStruct((flat, width), jnp.bfloat16),
        jax.ShapeDtypeStruct((flat, width), jnp.bfloat16),
        jax.ShapeDtypeStruct((blocks, heads * sequences // blocks, 3 * dim, rows), jnp.bfloat16),
    ]
    count = len(operands)
    return pl.pallas_call(
        partial(front_kernel, sequences=sequences, rows=rows, heads=heads, dim=dim, count=count),
        in_specs=[IN_HBM] * count,
        out_specs=[IN_HBM] * len(outs),
        out_shape=outs,
        scratch_shapes=held_here(operands) + held_here(outs) + [
            pltpu.VMEM((8 + rows, width), jnp.float32), pltpu.SemaphoreType.DMA((count + 6,)),
        ],
        compiler_params=pltpu.CompilerParams(vmem_limit_bytes=VMEM_LIMIT),
        cost_estimate=lasting(3.8),
        name="front",
    )(*operands)


def joined_blocks(ref, unit, first, count, low, high):
    return jnp.concatenate(
        [ref[first + i, unit, low:high, :] for i in range(count)], axis=1
    )


def unit_head(held, sequences):
    return (lax.axis_index("blk") * held + pl.program_id(0)) // sequences


def attend_kernel(
    qkv_ref, bucket_ref, table_ref, weight_ref, low_ref, att_ref, total_ref, toep_ref, key_ref,
    *, blocks, rows, dim, tile, held, sequences,
):
    length = blocks * rows
    step = pl.program_id(1)
    per_tile = tile // rows

    @pl.when(step == 0)
    def _():
        buckets = table_ref.shape[1]
        hot = lax.broadcasted_iota(jnp.int32, (buckets, 2 * length), 0) == bucket_ref[...]
        own = lax.broadcasted_iota(jnp.int32, table_ref.shape, 0) == unit_head(held, sequences)
        row = jnp.sum(jnp.where(own, table_ref[...].astype(jnp.float32), 0.0), axis=0, keepdims=True)
        square = (buckets, buckets)
        same = lax.broadcasted_iota(jnp.int32, square, 0) == lax.broadcasted_iota(jnp.int32, square, 1)
        column = jnp.sum(jnp.where(same, row, 0.0), axis=1, keepdims=True)
        line = jnp.sum(jnp.where(hot, column, 0.0), axis=0, keepdims=True)
        spread_line = jnp.broadcast_to(line, (rows, 2 * length))
        toep_ref[...] = pltpu.roll(spread_line, 0, 1, stride=1, stride_axis=0)
        for j in range(blocks):
            key_ref[rows * j : rows * (j + 1), :] = turned(qkv_ref[j, 0, dim : 2 * dim, :])

    query_t = joined_blocks(qkv_ref, 0, step * per_tile, per_tile, 0, dim)
    total = jnp.zeros((1, tile), jnp.float32)
    mix = jnp.zeros((dim, tile), jnp.float32)
    group = min(KEY_BLOCKS, blocks)
    for j in range(0, blocks, group):
        value_t = joined_blocks(qkv_ref, 0, j, group, 2 * dim, 3 * dim)
        bias = jnp.concatenate(
            [
                toep_ref[:, pl.ds(pl.multiple_of(length - rows + step * tile - rows * i, LANES), tile)]
                for i in range(j, j + group)
            ],
            axis=0,
        )
        span = slice(rows * j, rows * (j + group))
        weight = jnp.exp(project(key_ref[span, :], query_t) + bias)
        total = total + jnp.sum(weight, axis=0, keepdims=True)
        weight_low = weight.astype(jnp.bfloat16)
        weight_ref[0, span, :] = weight_low
        mix = mix + project(value_t, weight_low)
    att = mix / total
    att_ref[0] = att
    total_ref[0] = total
    att_low = att.astype(jnp.bfloat16)
    for i in range(per_tile):
        low_ref[i, 0] = att_low[:, i * rows : (i + 1) * rows]


def attend_back_kernel(
    qkv_ref, weight_ref, att_ref, total_ref, grad_ref, bucket_ref, out_ref, table_ref,
    diag_ref, gkey_ref, gvalue_ref, value_ref, *, blocks, rows, dim, tile, held, sequences,
):
    length = blocks * rows
    step = pl.program_id(1)
    per_tile = tile // rows

    @pl.when(step + pl.program_id(0) == 0)
    def _():
        table_ref[...] = jnp.zeros_like(table_ref)

    @pl.when(step == 0)
    def _():
        diag_ref[...] = jnp.zeros_like(diag_ref)
        gkey_ref[...] = jnp.zeros_like(gkey_ref)
        gvalue_ref[...] = jnp.zeros_like(gvalue_ref)
        for j in range(blocks):
            value_ref[rows * j : rows * (j + 1), :] = turned(qkv_ref[j, 0, 2 * dim : 3 * dim, :])

    query_t = joined_blocks(qkv_ref, 0, step * per_tile, per_tile, 0, dim)
    query = jnp.transpose(query_t.astype(jnp.float32)).astype(jnp.bfloat16)
    grad_att = joined_blocks(grad_ref, 0, 0, per_tile, 0, dim).astype(jnp.float32)
    inverse = 1.0 / total_ref[0]
    shift = jnp.sum(grad_att * att_ref[0], axis=0, keepdims=True) * inverse
    scaled = grad_att * inverse
    mix_t = scaled.astype(jnp.bfloat16)
    mix = jnp.transpose(scaled).astype(jnp.bfloat16)
    gquery = jnp.zeros((dim, tile), jnp.float32)
    group = min(KEY_BLOCKS, blocks)
    for j in range(0, blocks, group):
        span = slice(rows * j, rows * (j + group))
        key_t = joined_blocks(qkv_ref, 0, j, group, dim, 2 * dim)
        weight_low = weight_ref[0, span, :]
        grad_weight = project(value_ref[span, :], mix_t)
        grad_score = weight_low.astype(jnp.float32) * (grad_weight - shift)
        score_low = grad_score.astype(jnp.bfloat16)
        for i in range(group):
            start = pl.multiple_of(length - rows + step * tile - rows * (j + i), LANES)
            diag_ref[:, pl.ds(start, tile)] += grad_score[rows * i : rows * (i + 1)]
        gquery = gquery + project(key_t, score_low)
        gkey_ref[span, :] += project(score_low, query)
        gvalue_ref[span, :] += project(weight_low, mix)
    gquery_low = gquery.astype(jnp.bfloat16)
    for i in range(per_tile):
        out_ref[step * per_tile + i, 0, 0:dim, :] = gquery_low[:, i * rows : (i + 1) * rows]

    @pl.when(step == pl.num_programs(1) - 1)
    def _():
        for j in range(blocks):
            span = slice(rows * j, rows * (j + 1))
            out_ref[j, 0, dim : 2 * dim, :] = jnp.transpose(gkey_ref[span, :]).astype(jnp.bfloat16)
            out_ref[j, 0, 2 * dim : 3 * dim, :] = jnp.transpose(gvalue_ref[span, :]).astype(
                jnp.bfloat16
            )
        width = 2 * length
        part = diag_ref[...]
        half = rows // 2
        while half >= 8:
            part = part[:half] + pltpu.roll(part[half:], width - half, 1)
            half //= 2
        line = part[0:1]
        for r in range(1, 8):
            line = line + pltpu.roll(part[r : r + 1], width - r, 1)
        buckets = table_ref.shape[0]
        hot = lax.broadcasted_iota(jnp.int32, (buckets, width), 0) == bucket_ref[...]
        sums = jnp.sum(jnp.where(hot, line, 0.0), axis=1, keepdims=True)
        own = lax.broadcasted_iota(jnp.int32, table_ref.shape, 1) == unit_head(held, sequences)
        table_ref[...] += jnp.where(own, sums, 0.0)


def attend(qkv, bucket_line, table, blocks, rows, dim, tile, sequences):
    units = qkv.shape[1]
    length = blocks * rows
    per_tile = tile // rows
    return pl.pallas_call(
        partial(
            attend_kernel, blocks=blocks, rows=rows, dim=dim, tile=tile, held=units, sequences=sequences
        ),
        grid=(units, length // tile),
        in_specs=[
            pl.BlockSpec((blocks, 1, 3 * dim, rows), lambda u, i: (0, u, 0, 0)),
            pl.BlockSpec((1, 2 * length), lambda u, i: (0, 0)),
            whole(table.shape),
        ],
        out_specs=[
            pl.BlockSpec((1, length, tile), lambda u, i: (u, 0, i)),
            pl.BlockSpec((per_tile, 1, dim, rows), lambda u, i: (i, u, 0, 0)),
            pl.BlockSpec((1, dim, tile), lambda u, i: (u, 0, i)),
            pl.BlockSpec((1, 1, tile), lambda u, i: (u, 0, i)),
        ],
        out_shape=[
            jax.ShapeDtypeStruct((units, length, length), jnp.bfloat16),
            jax.ShapeDtypeStruct((blocks, units, dim, rows), jnp.bfloat16),
            jax.ShapeDtypeStruct((units, dim, length), jnp.float32),
            jax.ShapeDtypeStruct((units, 1, length), jnp.float32),
        ],
        scratch_shapes=[
            pltpu.VMEM((rows, 2 * length), jnp.float32), pltpu.VMEM((length, dim), jnp.bfloat16),
        ],
        compiler_params=pltpu.CompilerParams(vmem_limit_bytes=VMEM_LIMIT),
        cost_estimate=lasting(7),
        name="attend",
    )(qkv, bucket_line, table)


def attend_back(
    qkv, weight, att, total, grad_att, bucket_line, buckets, blocks, rows, dim, tile, sequences
):
    units = qkv.shape[1]
    length = blocks * rows
    per_tile = tile // rows
    return pl.pallas_call(
        partial(
            attend_back_kernel, blocks=blocks, rows=rows, dim=dim, tile=tile, held=units,
            sequences=sequences,
        ),
        grid=(units, length // tile),
        in_specs=[
            pl.BlockSpec((blocks, 1, 3 * dim, rows), lambda u, i: (0, u, 0, 0)),
            pl.BlockSpec((1, length, tile), lambda u, i: (u, 0, i)),
            pl.BlockSpec((1, dim, tile), lambda u, i: (u, 0, i)),
            pl.BlockSpec((1, 1, tile), lambda u, i: (u, 0, i)),
            pl.BlockSpec((per_tile, 1, dim, rows), lambda u, i: (i, u, 0, 0)),
            pl.BlockSpec((1, 2 * length), lambda u, i: (0, 0)),
        ],
        out_specs=[
            pl.BlockSpec((blocks, 1, 3 * dim, rows), lambda u, i: (0, u, 0, 0)),
            whole((buckets, LANES)),
        ],
        out_shape=[
            jax.ShapeDtypeStruct((blocks, units, 3 * dim, rows), jnp.bfloat16),
            jax.ShapeDtypeStruct((buckets, LANES), jnp.float32),
        ],
        scratch_shapes=[
            pltpu.VMEM((rows, 2 * length), jnp.float32),
            pltpu.VMEM((length, dim), jnp.float32),
            pltpu.VMEM((length, dim), jnp.float32),
            pltpu.VMEM((length, dim), jnp.bfloat16),
        ],
        compiler_params=pltpu.CompilerParams(vmem_limit_bytes=VMEM_LIMIT),
        cost_estimate=lasting(12),
        name="attend_back",
    )(qkv, weight, att, total, grad_att, bucket_line)


def unit_columns(parts_ref, sequences, heads, low, high):
    held = parts_ref.shape[1]

    def part(unit):
        return parts_ref[unit // held, unit % held, low:high, :]

    return jnp.concatenate(
        [
            jnp.concatenate([part(h * sequences + s) for h in range(heads)], axis=0)
            for s in range(sequences)
        ],
        axis=1,
    )


def middle_kernel(*refs, sequences, rows, heads, dim, count, chunks):
    given, made, held = refs[:count], refs[count : count + 7], refs[count + 7 : 2 * count + 7]
    out_ref, normed_ref, keep_ref, send_ref, gmid_ref, gsent_ref, ggain_ref = refs[2 * count + 7 : 2 * count + 14]
    total_ref, gnormed_ref, sems = refs[2 * count + 14 :]
    parts_ref, joined_ref, wout_ref, gain_ref, grad_ref, wgate_ref, wup_ref, wdown_ref = held
    half = chunks // 2
    piece = wgate_ref.shape[1] // chunks
    first = lax.axis_index("batch") % 2 * half
    spans = [pl.ds(pl.multiple_of((first + i) % chunks * piece, piece), piece) for i in range(chunks)]
    waiting = copies_between(given[:5], held[:5], sems)
    for i, span in enumerate(spans):
        pairs = [(given[5].at[:, span], wgate_ref.at[:, span]), (given[6].at[:, span], wup_ref.at[:, span]),
                 (given[7].at[span, :], wdown_ref.at[span, :])]
        waiting += copies_between([a for a, _ in pairs], [b for _, b in pairs], sems, 5 + 3 * i)
    used = 5 + 3 * chunks
    done = []

    def give(targets, sources):
        done.extend(copies_between(sources, targets, sems, used + len(done)))

    for copy in waiting[:5]:
        copy.wait()
    gain = gain_ref[...].astype(jnp.float32).reshape(1, -1)
    grad = grad_ref[...]
    att = turned(unit_columns(parts_ref, sequences, heads, 0, dim))
    mid = joined_ref[...] + project(att, wout_ref[...])
    joined_ref[...] = mid
    normed = (mid * inverse_rms(mid) * gain).astype(jnp.bfloat16)
    normed_ref[...] = normed
    give((made[1],), (normed_ref,))
    total_ref[...] = mid
    gnormed_ref[...] = jnp.zeros_like(gnormed_ref)
    for i, span in enumerate(spans):
        for copy in waiting[5 + 3 * i : 8 + 3 * i]:
            copy.wait()
        wgate, wup, wdown = wgate_ref[:, span], wup_ref[:, span], wdown_ref[span, :]
        gate = project(normed, wgate)
        up = project(normed, wup)
        square = gate * gate
        bend = jnp.tanh(GELU_SCALE * gate * (1.0 + GELU_CUBE * square))
        half_up = 0.5 + 0.5 * bend
        gelu = gate * half_up
        slope = half_up + 0.5 * gate * (1.0 - bend * bend) * (
            GELU_SCALE + (3.0 * GELU_SCALE * GELU_CUBE) * square
        )
        hidden = (gelu * up).astype(jnp.bfloat16)
        total_ref[...] += project(hidden, wdown)
        ghidden = project_back(grad, wdown)
        ggate = (ghidden * up * slope).astype(jnp.bfloat16)
        gup = (ghidden * gelu).astype(jnp.bfloat16)
        ref, target = (keep_ref, made[2]) if i < half else (send_ref, made[3])
        for part, block in enumerate((ggate, gup, hidden)):
            ref[i % half, part] = block
        give((target.at[i % half],), (ref.at[i % half],))
        gnormed_ref[...] += project_back(ggate, wgate) + project_back(gup, wup)
    out_ref[...] = total_ref[...].astype(jnp.bfloat16)
    give((made[0],), (out_ref,))
    back, ggain = rms_back(joined_ref[...], gain, gnormed_ref[...])
    gmid = grad.astype(jnp.float32) + back
    gmid_ref[...] = gmid
    ggain_ref[...] = ggain
    give((made[4], made[6]), (gmid_ref, ggain_ref))
    gatt = project_back(wout_ref[...], gmid.astype(jnp.bfloat16)).astype(jnp.bfloat16)
    for h in range(heads):
        for s in range(sequences):
            unit = h * sequences + s
            per_block = gsent_ref.shape[1]
            gsent_ref[unit // per_block, unit % per_block] = gatt[
                h * dim : (h + 1) * dim, s * rows : (s + 1) * rows
            ]
    give((made[5],), (gsent_ref,))
    for copy in done:
        copy.wait()


def middle(parts, joined, w_out, gain, w_gate, w_up, w_down, grad, sequences, heads, chunks):
    dim, rows = parts.shape[2:]
    flat, width = joined.shape
    piece = w_gate.shape[1] // chunks
    acts = (chunks // 2, 3, flat, piece)
    operands = (parts, joined, w_out, gain, grad, w_gate, w_up, w_down)
    outs = [
        jax.ShapeDtypeStruct((flat, width), jnp.bfloat16),
        jax.ShapeDtypeStruct((flat, width), jnp.bfloat16),
        jax.ShapeDtypeStruct(acts, jnp.bfloat16),
        jax.ShapeDtypeStruct(acts, jnp.bfloat16),
        jax.ShapeDtypeStruct((flat, width), jnp.float32),
        jax.ShapeDtypeStruct(parts.shape, jnp.bfloat16),
        jax.ShapeDtypeStruct((1, width), jnp.float32),
    ]
    count = len(operands)
    return pl.pallas_call(
        partial(
            middle_kernel, sequences=sequences, rows=rows, heads=heads, dim=dim, count=count, chunks=chunks
        ),
        in_specs=[IN_HBM] * count,
        out_specs=[IN_HBM] * len(outs),
        out_shape=outs,
        scratch_shapes=held_here(operands) + held_here(outs) + [
            pltpu.VMEM((flat, width), jnp.float32), pltpu.VMEM((flat, width), jnp.float32),
            pltpu.SemaphoreType.DMA((5 + 3 * chunks + 6 + chunks,)),
        ],
        compiler_params=pltpu.CompilerParams(vmem_limit_bytes=VMEM_LIMIT),
        cost_estimate=lasting(10),
        name="middle",
    )(*operands)


def halving_steps(flip):
    across, bit = [], 2
    while bit < lax.axis_size("batch"):
        across.append(("batch", bit))
        bit *= 2
    return [("blk", 1)] + across if flip else across + [("blk", 1)]


def group_of(steps, position):
    own = lax.axis_index("batch") // 2 * 2 + lax.axis_index("blk") % 2
    mask = 0
    for i, (axis, bit) in enumerate(steps):
        if position >> (len(steps) - 1 - i) & 1:
            mask += bit if axis == "batch" else 1
    return own ^ mask


def weights_kernel(*refs, steps):
    given, made, held = refs[:6], refs[6:10], refs[10:16]
    ready, square_ref, sems = refs[16:20], refs[20], refs[21]
    waiting = copies_between(given, held, sems)
    normed_ref, other_normed_ref, acts_ref, other_acts_ref, grad_ref, other_grad_ref = held
    half, lines, rows, _ = ready[0].shape
    width = square_ref.shape[1]
    span = lines * rows
    done = []

    def store(piece, part, square):
        square_ref[...] = square
        columns = slice(part * width, (part + 1) * width)
        pair = ready[2 * piece : 2 * piece + 2]
        for position in range(2 * half):
            first = pl.multiple_of(group_of(steps[piece], position) * span, span)
            shards = square_ref[pl.ds(first, span), :].astype(jnp.bfloat16).reshape(lines, rows, width)
            pair[position // half][position % half, :, :, columns] = shards
        done.extend(
            copies_between(
                [ref.at[:, :, :, pl.ds(part * width, width)] for ref in pair],
                [ref.at[:, :, :, pl.ds(part * width, width)] for ref in made[2 * piece : 2 * piece + 2]],
                sems,
                6 + len(done),
            )
        )

    for copy in waiting[:4]:
        copy.wait()
    normed_t, other_t = turned(normed_ref[...]), turned(other_normed_ref[...])
    for piece in range(2):
        for part in range(2):
            store(
                piece, part,
                project(normed_t, acts_ref[piece, part]) + project(other_t, other_acts_ref[piece, part]),
            )
        if piece == 0:
            for copy in waiting[4:]:
                copy.wait()
        store(
            piece, 2,
            over_rows(acts_ref[piece, 2], grad_ref[...])
            + over_rows(other_acts_ref[piece, 2], other_grad_ref[...]),
        )
    for copy in done:
        copy.wait()


def weight_grads(acts, normed, grad, shape, steps):
    width = normed[0].shape[1]
    count = acts[0].shape[1]
    rows = width // (shape[0] * shape[1])
    block = (shape[0] // 2, shape[1], rows, count * width)
    operands = (*normed, *acts, *grad)
    outs = [jax.ShapeDtypeStruct(block, jnp.bfloat16)] * 4
    return pl.pallas_call(
        partial(weights_kernel, steps=steps),
        in_specs=[IN_HBM] * 6,
        out_specs=[IN_HBM] * 4,
        out_shape=outs,
        scratch_shapes=held_here(operands) + held_here(outs) + [
            pltpu.VMEM((width, width), jnp.float32), pltpu.SemaphoreType.DMA((6 + 4 * count,)),
        ],
        compiler_params=pltpu.CompilerParams(vmem_limit_bytes=VMEM_LIMIT),
        cost_estimate=lasting(6),
        name="weight_grads",
    )(*operands)


def grid_of():
    return lax.axis_size("batch"), lax.axis_size("blk") // 2


def place_square(keep_ref, send_ref, square, start, shape):
    width = square.shape[1]
    half = square.shape[0] // 2
    columns = slice(start, start + width)
    parity = lax.axis_index("batch") % 2
    for h in range(2):
        shards = square[h * half : (h + 1) * half].astype(jnp.bfloat16).reshape(shape + (-1, width))

        @pl.when(parity == h)
        def _():
            keep_ref[:, :, :, columns] = shards

        @pl.when(parity != h)
        def _():
            send_ref[:, :, :, columns] = shards


def held_here(shapes):
    return [pltpu.VMEM(a.shape, a.dtype) for a in shapes]


def copies_between(sources, targets, sems, first=0):
    copies = [
        pltpu.make_async_copy(source, target, sems.at[first + i])
        for i, (source, target) in enumerate(zip(sources, targets))
    ]
    for copy in copies:
        copy.start()
    return copies


def last_kernel(*refs, sequences, rows, heads, dim, shape, count):
    width = heads * dim
    given, made, held = refs[:count], refs[count : count + 4], refs[count + 4 : 2 * count + 4]
    keep_ref, send_ref, gstates_ref, spill_ref, ext_ref, sems = refs[2 * count + 4 :]
    waiting = copies_between(given, held, sems)
    (parts_ref, normed_ref, wq_ref, wk_ref, wv_ref, att_ref, gmid_ref, joined_ref, gain_ref, ngram_ref, wjoin_ref,
     states_ref, rim_ref, start_ref, two_ref, three_ref, four_ref, ggain_ffn_ref, table_ref) = held
    done = []

    def need(*names):
        for index in names:
            waiting[index].wait()

    def give(targets, sources):
        done.extend(copies_between(sources, targets, sems, count + len(done)))

    def store(square, start):
        place_square(keep_ref, send_ref, square, start, shape)
        columns = pl.ds(start, square.shape[1])
        give(
            [ref.at[:, :, :, columns] for ref in made[:2]],
            [ref.at[:, :, :, columns] for ref in (keep_ref, send_ref)],
        )

    need(0, 1)
    normed_t = turned(normed_ref[...])
    gnormed = jnp.zeros(joined_ref.shape, jnp.float32)
    for part, w_ref in enumerate((wq_ref, wk_ref, wv_ref)):
        low = part * dim
        grad = turned(unit_columns(parts_ref, sequences, heads, low, low + dim))
        store(project(normed_t, grad), part * width)
        need(2 + part)
        gnormed = gnormed + project_back(grad, w_ref[...])
    need(5, 6)
    att_t = unit_columns(att_ref, sequences, heads, 0, dim)
    store(project(att_t, gmid_ref[...].astype(jnp.bfloat16)), 4 * width)
    need(7, 8)
    back, ggain = rms_back(
        joined_ref[...], gain_ref[...].astype(jnp.float32).reshape(1, -1), gnormed
    )
    gjoined = gmid_ref[...] + back
    gjoined_low = gjoined.astype(jnp.bfloat16)
    need(9)
    store(over_rows(ngram_ref[...], gjoined_low), 3 * width)
    need(*range(10, count))
    gngram = project_back(gjoined_low, wjoin_ref[...])
    taps = tap_rows(two_ref, three_ref, four_ref)
    gtaps = [jnp.zeros((1, width), jnp.float32)] * 4
    for s in range(sequences):
        span = slice(s * rows, (s + 1) * rows)
        states = states_ref[s].astype(jnp.float32)
        keeps = keep_columns(start_ref, s, lax.axis_index("blk") * rows, rows, width)
        ext_ref[8 - EDGE : 8, :] = rim_ref[s].astype(jnp.float32)
        ext_ref[8 : 8 + rows, :] = states
        masked = [keeps[j] * gngram[span] for j in range(4)]
        for j in range(4):
            moved = states if j == 0 else ext_ref[8 - j : 8 - j + rows, :]
            gtaps[j] = gtaps[j] + jnp.sum(masked[j] * moved, axis=0, keepdims=True)
        ext_ref[...] = jnp.zeros_like(ext_ref)
        ext_ref[8 : 8 + rows, :] = gjoined[span] + taps[0] * masked[0]
        for j in range(1, 4):
            ext_ref[8 - j : 8 - j + rows, :] += taps[j] * masked[j]
        gstates_ref[s] = ext_ref[8 : 8 + rows, :]
        spill_ref[s] = ext_ref[0:8, :]
    small = jnp.concatenate(gtaps + [ggain, ggain_ffn_ref[...], jnp.zeros((2, width), jnp.float32)], axis=0)
    lines = jnp.concatenate(
        [small[:, i * LANES : (i + 1) * LANES] for i in range(width // LANES)] + [table_ref[...]], axis=0
    )
    lines = jnp.concatenate([lines, jnp.zeros((width - lines.shape[0], LANES), jnp.float32)], axis=0)
    store(lines, 5 * width)
    give(made[2:], (gstates_ref, spill_ref))
    for copy in done:
        copy.wait()


def last(parts, att_parts, normed, joined, gmid, ngram, states, rim, starts, two, three, four,
         w_join, gain, w_query, w_key, w_value, ggain_ffn, table, heads, shape):
    sequences, rows, width = states.shape
    dim = width // heads
    shards = shape + (width // (2 * shape[0] * shape[1]), 5 * width + LANES)
    operands = (parts, normed, w_query, w_key, w_value, att_parts, gmid, joined, gain, ngram, w_join,
                states, rim, starts, two, three, four, ggain_ffn, table)
    outs = [
        jax.ShapeDtypeStruct(shards, jnp.bfloat16),
        jax.ShapeDtypeStruct(shards, jnp.bfloat16),
        jax.ShapeDtypeStruct((sequences, rows, width), jnp.float32),
        jax.ShapeDtypeStruct((sequences, 8, width), jnp.float32),
    ]
    count = len(operands)
    return pl.pallas_call(
        partial(
            last_kernel, sequences=sequences, rows=rows, heads=heads, dim=dim, shape=shape, count=count
        ),
        in_specs=[IN_HBM] * count,
        out_specs=[IN_HBM] * len(outs),
        out_shape=outs,
        scratch_shapes=held_here(operands) + held_here(outs) + [
            pltpu.VMEM((8 + rows, width), jnp.float32), pltpu.SemaphoreType.DMA((count + 14,)),
        ],
        compiler_params=pltpu.CompilerParams(vmem_limit_bytes=VMEM_LIMIT),
        cost_estimate=lasting(7),
        name="last",
    )(*operands)


def unplace_half(source, targets, held, ready, sems, side):
    count, width = len(targets), targets[0].shape[1]
    half = width // 2
    columns = [pl.ds(part * width, width) for part in range(count)]
    waiting = copies_between(
        [source.at[:, :, :, c] for c in columns], [held.at[:, :, :, c] for c in columns], sems
    )
    place = pl.ds(pl.multiple_of(side * half, half), half)
    done = []
    for part, (copy, target) in enumerate(zip(waiting, targets)):
        copy.wait()
        shards = held[:, :, :, part * width : (part + 1) * width].astype(jnp.float32)
        ready[part] = shards.reshape(half, width)
        done += copies_between((ready.at[part],), (target.at[place, :],), sems, count + part)
    return done


def unplace_own_kernel(own_ref, *refs, count):
    held, ready, sems = refs[count:]
    done = unplace_half(own_ref, refs[:count], held, ready, sems, lax.axis_index("batch") % 2)
    for copy in done:
        copy.wait()


def unplace_other_kernel(other_ref, own_lines_ref, *refs, count, buckets):
    outs = refs[count:]
    parity = lax.axis_index("batch") % 2
    width = outs[0].shape[1]
    for part, out in enumerate(outs[:count]):
        held = other_ref[:, :, :, part * width : (part + 1) * width].astype(jnp.float32)
        out[...] = held.reshape(out.shape)
    other_lines = other_ref[:, :, :, count * width :]
    lines = jnp.where(parity == 0, own_lines_ref[...], other_lines).astype(jnp.float32)
    lines = lines.reshape(-1, LANES)
    pieces = width // LANES
    small = jnp.concatenate([lines[8 * i : 8 * i + 8] for i in range(pieces)], axis=1)
    two, three, four, gain, gain_ffn, table = outs[count:]
    two[...], three[...], four[...] = small[0:2], small[0:3], small[0:4]
    gain[...], gain_ffn[...] = small[4:5], small[5:6]
    table[...] = jnp.transpose(lines[8 * pieces : 8 * pieces + buckets])[: table.shape[0]]


def half_scratch(shards, width, count):
    return held_here((shards,)) + [
        pltpu.VMEM((count, width // 2, width), jnp.float32), pltpu.SemaphoreType.DMA((2 * count,)),
    ]


def unplace_own(own, width, count):
    return pl.pallas_call(
        partial(unplace_own_kernel, count=count),
        in_specs=[IN_HBM],
        out_specs=[IN_HBM] * count,
        out_shape=[jax.ShapeDtypeStruct((width, width), jnp.float32)] * count,
        scratch_shapes=half_scratch(own, width, count),
        compiler_params=pltpu.CompilerParams(vmem_limit_bytes=VMEM_LIMIT),
        cost_estimate=lasting(2.5),
        name="unplace_own",
    )(own)


def unplace_other(other, own, squares, width, table_shape):
    count = len(squares)
    shapes = [(width, width)] * count
    shapes += [(2, width), (3, width), (4, width), (1, width), (1, width), table_shape]
    half = width // 2
    lines = pl.BlockSpec(own.shape[:3] + (LANES,), lambda i: (0, 0, 0, count * width // LANES))
    outs = [jax.ShapeDtypeStruct(shape, jnp.float32) for shape in shapes]
    parts = pl.BlockSpec((half, width), lambda i: (1 - lax.axis_index("batch") % 2, 0))
    return pl.pallas_call(
        partial(unplace_other_kernel, count=count, buckets=table_shape[1]),
        grid=(1,),
        in_specs=[whole(other.shape), lines] + [pl.BlockSpec(memory_space=pl.ANY)] * count,
        out_specs=[parts] * count + [whole(a.shape) for a in outs[count:]],
        out_shape=outs,
        input_output_aliases={2 + i: i for i in range(count)},
        compiler_params=pltpu.CompilerParams(vmem_limit_bytes=VMEM_LIMIT),
        cost_estimate=lasting(3),
        name="unplace_other",
    )(other, own, *squares)


def unplace_ffn_kernel(*refs, steps, count, given, piece, chunks):
    blocks, outs = refs[: 2 * count], refs[given : given + 3]
    held, ready, sems = refs[given + 3 : given + 3 + 2 * count], refs[given + 3 + 2 * count], refs[-1]
    waiting = copies_between(blocks, held, sems)
    lines, rows = held[0].shape[:2]
    width = ready.shape[-1]
    span = lines * rows
    done = []
    for side in range(2):
        for copy in waiting[side * count : (side + 1) * count]:
            copy.wait()
        chunk = (lax.axis_index("batch") + side) % 2 * (chunks // 2) + piece
        place = pl.ds(pl.multiple_of(chunk * width, width), width)
        for part in range(3):
            for i, block in enumerate(held[side * count : (side + 1) * count]):
                start = pl.multiple_of(group_of(steps, i) * span, span)
                shards = block[:, :, part * width : (part + 1) * width].astype(jnp.float32)
                ready[side, part, pl.ds(start, span), :] = shards.reshape(span, width)
            target = outs[part].at[place, :] if part == 2 else outs[part].at[:, place]
            done += copies_between((ready.at[side, part],), (target,), sems, 2 * count + len(done))
    for copy in done:
        copy.wait()


def unplace_ffn(blocks, steps, piece, width, hidden, chunks, before=()):
    shapes = [(width, hidden), (width, hidden), (hidden, width)]
    given = len(blocks) + len(before)
    return pl.pallas_call(
        partial(
            unplace_ffn_kernel, steps=steps, count=len(blocks) // 2, given=given, piece=piece, chunks=chunks
        ),
        in_specs=[IN_HBM] * given,
        out_specs=[IN_HBM] * 3,
        out_shape=[jax.ShapeDtypeStruct(shape, jnp.float32) for shape in shapes],
        input_output_aliases={len(blocks) + i: i for i in range(len(before))},
        scratch_shapes=held_here(blocks) + [
            pltpu.VMEM((2, 3, width, width), jnp.float32), pltpu.SemaphoreType.DMA((len(blocks) + 6,)),
        ],
        compiler_params=pltpu.CompilerParams(vmem_limit_bytes=VMEM_LIMIT),
        cost_estimate=lasting(4),
        name="unplace_ffn",
    )(*blocks, *before)


def to_line_kernel(*refs, first, second, lines):
    count = first + second
    given, made, held = refs[:count], refs[count : count + lines], refs[count + lines : 2 * count + lines]
    ready, sems = refs[2 * count + lines :]
    waiting = copies_between([ref.at[0] for ref in given], held, sems)
    wide = held[0].shape[-1]

    def total(terms):
        held_sum = terms[0][...].astype(jnp.float32)
        for term in terms[1:]:
            held_sum = held_sum + term[...].astype(jnp.float32)
        return held_sum.astype(jnp.bfloat16)

    for copy in waiting[:first]:
        copy.wait()
    ready[:, :, :wide] = total(held[:first])
    for copy in waiting[first:]:
        copy.wait()
    ready[:, :, wide:] = total(held[first:])
    own = lax.axis_index("blk") // 2
    done = copies_between([ready.at[own ^ d] for d in range(lines)], made, sems, count)
    for copy in done:
        copy.wait()


def to_line(first, second):
    lines, rows, wide = first[0].shape[1:]
    total = wide + second[0].shape[-1]
    operands = (*first, *second)
    count = len(operands)
    return pl.pallas_call(
        partial(to_line_kernel, first=len(first), second=len(second), lines=lines),
        in_specs=[IN_HBM] * count,
        out_specs=[IN_HBM] * lines,
        out_shape=[jax.ShapeDtypeStruct((rows, total), jnp.bfloat16)] * lines,
        scratch_shapes=[pltpu.VMEM(a.shape[1:], a.dtype) for a in operands] + [
            pltpu.VMEM((lines, rows, total), jnp.bfloat16), pltpu.SemaphoreType.DMA((count + lines,)),
        ],
        compiler_params=pltpu.CompilerParams(vmem_limit_bytes=VMEM_LIMIT),
        cost_estimate=lasting(3),
        name="to_line",
    )(*operands)


def from_line_kernel(*refs):
    first_ref, second_ref = refs[-2:]
    wide = first_ref.shape[-1]
    own = lax.axis_index("blk") // 2
    for d, piece in enumerate(refs[:-2]):
        first_ref[own ^ d] = piece[:, :wide]
        second_ref[own ^ d] = piece[:, wide:]


def from_line(pieces, wide):
    rows, total = pieces[0].shape
    shapes = [(len(pieces), rows, wide), (len(pieces), rows, total - wide)]
    return pl.pallas_call(
        from_line_kernel,
        grid=(1,),
        in_specs=[whole(a.shape) for a in pieces],
        out_specs=[whole(shape) for shape in shapes],
        out_shape=[jax.ShapeDtypeStruct(shape, jnp.bfloat16) for shape in shapes],
        compiler_params=pltpu.CompilerParams(vmem_limit_bytes=VMEM_LIMIT),
        cost_estimate=lasting(2),
        name="from_line",
    )(*pieces)


def traded(block, axis, bit):
    pairs = [(i, i ^ bit) for i in range(lax.axis_size(axis))]
    return lax.ppermute(block, axis, pairs)


def swapped(block):
    return traded(block, "batch", 1)


def line_traded(blocks):
    _, lines = grid_of()
    if not isinstance(blocks, (list, tuple)):
        blocks = [blocks] * (lines - 1)
    return [traded(block, "blk", 2 * (d + 1)) for d, block in enumerate(blocks)]


def added(*terms):
    total = terms[0].astype(jnp.float32)
    for term in terms[1:]:
        total = total + term.astype(jnp.float32)
    return total.astype(jnp.bfloat16)


def summed_first(parts):
    return lax.reduce(parts.astype(jnp.float32), jnp.float32(0), lax.add, (0,)).astype(jnp.bfloat16)


def over_plane(parts):
    batch, lines = grid_of()
    groups = [
        [(2 * line + p % 2) * batch + p // 2 * 2 + parity for p in range(batch)]
        for line in range(lines)
        for parity in range(2)
    ]
    return lax.all_to_all(parts, ("blk", "batch"), 0, 0, axis_index_groups=groups, tiled=True)


def over_line(parts):
    _, lines = grid_of()
    groups = [[2 * line + low for line in range(lines)] for low in range(2)]
    return lax.all_to_all(parts, "blk", 0, 0, axis_index_groups=groups, tiled=True)


def spread(block, count):
    return jnp.broadcast_to(block[None], (count,) + block.shape)


def spill_kernel(states_ref, spill_ref, out_ref):
    out_ref[...] = states_ref[...]
    for s in range(states_ref.shape[0]):
        out_ref[s, 8 - EDGE :, :] += spill_ref[s]


def add_spill(states, spill):
    sequences, rows, width = states.shape
    edge = pl.BlockSpec((sequences, 8, width), lambda i: (0, rows // 8 - 1, 0))
    return pl.pallas_call(
        spill_kernel,
        grid=(1,),
        in_specs=[edge, whole(spill.shape)],
        out_specs=edge,
        out_shape=jax.ShapeDtypeStruct(states.shape, states.dtype),
        input_output_aliases={0: 0},
        cost_estimate=lasting(1.4),
        name="add_spill",
    )(states, spill)


def exchanged(parts):
    return lax.all_to_all(parts, "blk", 0, 0, tiled=True)


def per_device(
    byte_states,
    word_start,
    bucket_of,
    conv_two,
    conv_three,
    conv_four,
    w_join,
    norm_attn,
    w_query,
    w_key,
    w_value,
    w_out,
    rel_bias,
    norm_ffn,
    w_gate,
    w_up,
    w_down,
    grad_output,
):
    sequences, block_rows, model_width = byte_states.shape
    blocks = lax.axis_size("blk")
    block_index = lax.axis_index("blk")
    head_count = rel_bias.shape[1]
    head_dim = model_width // head_count
    flat_rows = sequences * block_rows
    units = head_count * sequences
    held = units // blocks
    tile = 8 * block_rows
    shape = grid_of()
    plane, line = shape
    pin = lax.optimization_barrier
    grad_low = grad_output.reshape(flat_rows, model_width)
    other_grad = swapped(grad_low)
    rim_rows = shifted(byte_states[:, block_rows - EDGE :, :], "blk", 1)

    flipped = jnp.flip(bucket_of)
    near = block_rows - 1
    bucket_line = jnp.concatenate(
        [flipped[near:], jnp.zeros((1,), jnp.int32), flipped[:near]]
    )[None]
    joined, normed_attn, ngram_low, sent = front(
        byte_states, rim_rows, word_start, conv_two, conv_three, conv_four, w_join,
        norm_attn, w_query, w_key, w_value, head_count, blocks,
    )
    qkv = exchanged(sent)
    weight, att_sent, attended, total = attend(
        qkv, bucket_line, rel_bias.T, blocks, block_rows, head_dim, tile, sequences
    )
    att_parts = exchanged(att_sent)
    output, normed_ffn, keep_acts, send_acts, grad_mid, grad_att, ggain_ffn = middle(
        att_parts, joined, w_out, norm_ffn, w_gate, w_up, w_down, grad_low, sequences, head_count, CHUNKS
    )
    grad_parts = exchanged(grad_att)
    acts = (keep_acts, swapped(send_acts))
    normed_pair = (normed_ffn, swapped(normed_ffn))
    grad_pair = (grad_low, other_grad)
    steps_1, steps_2 = halving_steps(False), halving_steps(True)
    keep_1, out_1, keep_2, out_2 = weight_grads(acts, normed_pair, grad_pair, shape, (steps_1, steps_2))
    grad_parts, out_1, out_2 = pin((grad_parts, out_1, out_2))

    grad_qkv, grad_table = attend_back(
        qkv, weight, attended, total, grad_parts, bucket_line,
        rel_bias.shape[0], blocks, block_rows, head_dim, tile, sequences,
    )
    in_1, in_2 = traded(out_1, *steps_1[0]), traded(out_2, *steps_2[0])

    def to_send(held):
        half = held[-1].shape[0] // 2
        return added(*[h[half : 2 * half] for h in held])

    qkv_parts = exchanged(grad_qkv)
    held_1, held_2 = [keep_1, in_1], [keep_2, in_2]
    for step_1, step_2 in zip(steps_1[1:], steps_2[1:]):
        held_1.append(traded(to_send(held_1), *step_1))
        held_2.append(traded(to_send(held_2), *step_2))
    keep_3, send_3, grad_states, spill = last(
        qkv_parts, att_parts, normed_attn, joined, grad_mid, ngram_low, byte_states, rim_rows, word_start,
        conv_two, conv_three, conv_four, w_join, norm_attn, w_query, w_key, w_value, ggain_ffn,
        grad_table, head_count, shape,
    )
    send_3, held_1[-1], held_2[-1] = pin((send_3, held_1[-1], held_2[-1]))
    own_line, *out_line = to_line(held_1, held_2)
    got_3, own_line, out_line = pin((swapped(send_3), own_line, out_line))

    plane_3 = over_plane(added(keep_3, got_3))
    final = added(own_line, *line_traded(out_line))
    pieces = [final] + line_traded(final)
    plane_3, pieces = pin((plane_3, pieces))

    def gathered(held, axis, bit):
        return held + [traded(block, axis, bit) for block in held]

    def gathered_on(block, direct, steps):
        held = [block]
        for got, step in zip(direct, steps[::-1]):
            held = held + [got] + [traded(other, *step) for other in held[1:]]
        return held

    block_1, block_2 = from_line(pieces, keep_1.shape[-1])
    direct_1 = [traded(block_1, *step) for step in steps_1[::-1]]
    direct_2 = [traded(block_2, *step) for step in steps_2[::-1]]
    line_3 = over_line(summed_first(plane_3))
    direct_1, direct_2, spill = pin((direct_1, direct_2, spill))

    held_1 = gathered_on(block_1, direct_1, steps_1)
    held_2 = gathered_on(block_2, direct_2, steps_2)
    half_3 = spread(over_line(spread(summed_first(line_3), line)), plane)
    spill_rows = shifted(spill[:, 8 - EDGE :, :], "blk", -1)
    half_3, held_1, held_2, spill_rows = pin((half_3, held_1, held_2, spill_rows))
    grad_states = add_spill(grad_states, spill_rows)

    own_3 = over_plane(half_3)
    blocks_1, blocks_2 = gathered(held_1, "batch", 1), gathered(held_2, "batch", 1)
    ffn_sizes = (model_width, w_gate.shape[1], CHUNKS)
    halfway = unplace_ffn(blocks_1, steps_1, 0, *ffn_sizes)
    ffn_sums = unplace_ffn(blocks_2, steps_2, 1, *ffn_sizes, tuple(halfway))
    own_3, (gate_sum, up_sum, down_sum), grad_states = pin((own_3, tuple(ffn_sums), grad_states))

    other_3 = swapped(own_3)
    squares = unplace_own(own_3, model_width, 5)
    *squares, two, three, four, gain_sum, gain_ffn_sum, table_sum = unplace_other(
        other_3, own_3, squares, model_width, rel_bias.shape[::-1]
    )
    query_sum, key_sum, value_sum, join_sum, out_sum = squares
    return (
        output.reshape(byte_states.shape),
        grad_states,
        two,
        three,
        four,
        join_sum,
        gain_sum[0],
        query_sum,
        key_sum,
        value_sum,
        out_sum,
        table_sum.T,
        gain_ffn_sum[0],
        gate_sum,
        up_sum,
        down_sum,
    )


def solution(mesh):
    return jax.shard_map(
        per_device,
        mesh=mesh,
        in_specs=(
            P("batch", "blk", None),
            P("batch", "blk"),
            P(),
            P(),
            P(),
            P(),
            P(),
            P(),
            P(),
            P(),
            P(),
            P(),
            P(),
            P(),
            P(),
            P(),
            P(),
            P("batch", "blk", None),
        ),
        out_specs=(
            P("batch", "blk", None),
            P("batch", "blk", None),
            P(),
            P(),
            P(),
            P(),
            P(),
            P(),
            P(),
            P(),
            P(),
            P(),
            P(),
            P(),
            P(),
            P(),
        ),
        check_vma=False,
    )
```

time: 2220 us -> 228 us (0.10)
  local copies, waits for them, and re-layouts: 1540 us -> 5.51 us
  waiting for transfers between devices: 451 us -> 78.8 us
  matrix products: 113 us -> 0 us
  Pallas kernels: 0 us -> 56.7 us
  starting transfers between devices: 10.6 us -> 63.5 us
  blocking collectives: 41.1 us -> 12.5 us
  other arithmetic: 37.2 us -> 8.96 us
    gather x10 -> x0, local copies, waits for them, and re-layouts: 1450 us -> none  [bias_block(): jnp.take(bucket_of, key_pos[None, :] - query_pos[:, None] + length - 1)]
    psum x1 -> x0, waiting for transfers between devices: 231 us -> none  [per_device(): lax.psum((grad_conv_two, grad_conv_three, grad_conv_four, grad_w_join, gr...]
    ppermute x15 -> x29, waiting for transfers between devices: 219 us -> 37.7 us  [traded(): return lax.ppermute(block, axis, pairs)]
    dot_general x83 -> x0, matrix products: 113 us -> none  [the longest x8 18.1 us: key_grads(): jnp.einsum('sqhd,skhd->shqk', grad_mix, value_heads, preferred_element_ty...]
    pallas_call x0 -> x13, Pallas kernels: none -> 56.7 us  [the longest x2 8.48 us: unplace_ffn(): pl.pallas_call(partial(unplace_ffn_kernel, steps=steps, count=len(blocks)...]
    psum x1 -> x0, blocking collectives: 41.1 us -> none  [per_device(): lax.psum((grad_conv_two, grad_conv_three, grad_conv_four, grad_w_join, gr...]
    all_to_all x0 -> x7, waiting for transfers between devices: none -> 32.6 us  [the longest x3 26.8 us: exchanged(): return lax.all_to_all(parts, 'blk', 0, 0, tiled=True)]
    all_to_all x0 -> x7, starting transfers between devices: none -> 31 us  [the longest x3 15.2 us: exchanged(): return lax.all_to_all(parts, 'blk', 0, 0, tiled=True)]
  transfers between devices with their start and end apart: 19 -> 38, of which waited for: 9 -> 20; matrix products, arithmetic and copies ran while one was open for 40% -> 4% of each run, Pallas kernels for 0% -> 16%
where the time goes in v1:
time: 228 us; the launch traced here: 227 us
  waiting for transfers between devices  78.8 us (35%)
  starting transfers between devices  63.5 us (28%)
  Pallas kernels  56.7 us (25%)
  blocking collectives  12.5 us (5%)
  other arithmetic  8.96 us (4%)
  local copies, waits for them, and re-layouts  5.51 us (2%)
    ppermute x29, waiting for transfers between devices, traded(): return lax.ppermute(block, axis, pairs)  37.7 us
    all_to_all x3, waiting for transfers between devices, exchanged(): return lax.all_to_all(parts, 'blk', 0, 0, tiled=True)  26.8 us
    ppermute x29, starting transfers between devices, traded(): return lax.ppermute(block, axis, pairs)  26.4 us
    all_to_all x3, starting transfers between devices, exchanged(): return lax.all_to_all(parts, 'blk', 0, 0, tiled=True)  15.2 us
    all_to_all x1, blocking collectives, exchanged(): return lax.all_to_all(parts, 'blk', 0, 0, tiled=True)  12.5 us
    pallas_call x2, Pallas kernels, unplace_ffn(): pl.pallas_call(partial(unplace_ffn_kernel, steps=steps, count=len(blocks)...  8.48 us
    ppermute x2, waiting for transfers between devices, shifted(): return lax.ppermute(block, axis, route)  8.47 us
    pallas_call x1, Pallas kernels, attend_back(): pl.pallas_call(partial(attend_back_kernel, blocks=blocks, rows=rows, dim=...  8.14 us
  transfers between devices with their start and end apart: 38, of which 20 were waited for; matrix products, arithmetic and copies ran while one was open for 4% of the time, Pallas kernels for 16%

profile of v1, /device:TPU:0, one launch (start us, length us, event | category | flops | bytes accessed | tf_op | source)
XLA Modules:
  0.0 227.0 jit_solution(12683101440646783440)
XLA Ops:
  1.4 4.8 %collective-permute-start = (bf16[2,3,512]{2,1,0:T(4,128)(2,1)S(1)}, bf16[2,3,512]{2,1,0:T(4,128)(2,1)S(1)}, u32[]{:S(2)}, u32[]{:S(2)}) collective-permute-start(bf16[2,3,512]{2,1,0:T(4,128)(2,1)S(1)} %slice.30), channel_id=1, source_target_pairs={{0,4},{4,8},{8,12},{12,16},{16,20},{20,24},{24,28},{1,5},{5,9},{9,... | collective-permute-start | bytes 18440 | tf_op jit(solution)/shard_map/ppermute | solution.py:30
  11.9 6.6 %all-to-all-start = ((bf16[8,2,192,128]{3,2,1,0:T(8,128)(2,1)}), bf16[8,2,192,128]{3,2,1,0:T(8,128)(2,1)}, u32[]{:S(2)}, u32[]{:S(2)}) async-start(bf16[8,2,192,128]{3,2,1,0:T(8,128)(2,1)} %get-tuple-element.105), calls=%async_computation | async-start | bytes 1572864 | tf_op jit(solution)/shard_map/all_to_all | solution.py:984
  19.4 18.3 %all-to-all-done.qkv_ref = bf16[8,2,192,128]{3,2,1,0:T(8,128)(2,1)} async-done(((bf16[8,2,192,128]{3,2,1,0:T(8,128)(2,1)}), bf16[8,2,192,128]{3,2,1,0:T(8,128)(2,1)}, u32[]{:S(2)}, u32[]{:S(2)}) %all-to-all-start) | async-done | bytes 786464 | tf_op jit(solution)/shard_map/all_to_all | solution.py:984
  37.7 5.2 %attend.1 = (bf16[2,1024,1024]{2,1,0:T(8,128)(2,1)}, bf16[8,2,64,128]{3,2,1,0:T(8,128)(2,1)}, f32[2,64,1024]{2,1,0:T(8,128)}, f32[2,1,1024]{2,1,0:T(1,128)}) custom-call(bf16[8,2,192,128]{3,2,1,0:T(8,128)(2,1)} %all-to-all-done.qkv_ref, s32[1,2048]{1,0:T(1,128)} %bitcast.11, bf16[8,32]{1,0:T(8,128)(2,1)} %bitcast.14), custom_call_target="tpu_custom_call" | custom-call | bytes 24500000 | tf_op jit(solution)/shard_map/attend/pallas_call | solution.py:301
  43.0 12.5 %all_to_all.40.refs_0_.refs_5_ = bf16[8,2,64,128]{3,2,1,0:T(8,128)(2,1)} all-to-all(bf16[8,2,64,128]{3,2,1,0:T(8,128)(2,1)} %get-tuple-element.106), channel_id=1, replica_groups=mesh['blk'=8,'batch'=4] {'blk'}, dimensions={0} | all-to-all | bytes 524288 | tf_op jit(solution)/shard_map/all_to_all | solution.py:984
  55.5 7.8 %middle.1 = (bf16[256,512]{1,0:T(8,128)(2,1)}, bf16[256,512]{1,0:T(8,128)(2,1)}, bf16[2,3,256,512]{3,2,1,0:T(8,128)(2,1)}, bf16[2,3,256,512]{3,2,1,0:T(8,128)(2,...) custom-call(bf16[8,2,64,128]{3,2,1,0:T(8,128)(2,1)} %all_to_all.40.refs_0_.refs_5_, ...), custom_call_target="tpu_custom_call" | custom-call | bytes 35000000 | tf_op jit(solution)/shard_map/middle/pallas_call | solution.py:478
  63.4 4.2 %all-to-all-start.2 = ((bf16[8,2,64,128]{3,2,1,0:T(8,128)(2,1)}), bf16[8,2,64,128]{3,2,1,0:T(8,128)(2,1)}, u32[]{:S(2)}, u32[]{:S(2)}) async-start(bf16[8,2,64,128]{3,2,1,0:T(8,128)(2,1)} %get-tuple-element.112), calls=%async_computation.2 | async-start | bytes 524288 | tf_op jit(solution)/shard_map/all_to_all | solution.py:984
  70.1 5.2 %weight_grads.1 = (bf16[2,4,32,1536]{3,2,1,0:T(8,128)(2,1)}, bf16[2,4,32,1536]{3,2,1,0:T(8,128)(2,1)}, bf16[2,4,32,1536]{3,2,1,0:T(8,128)(2,1)}, bf16[2,4,32,1536]{3,2,1,0:T(8,128)(2,1)}) custom-call(bf16[256,512]{1,0:T(8,128)(2,1)} %get-tuple-element.113.refs_0_, bf16[256,512]{1,0:T(8,128)(2,1)} %collective-permute-done.1.refs_1_, ...), custom_call_target="tpu_custom_call" | custom-call | bytes 21000000 | tf_op jit(solution)/shard_map/weight_grads/pallas_call | solution.py:567
  80.2 8.1 %attend_back.1 = (bf16[8,2,192,128]{3,2,1,0:T(8,128)(2,1)}, f32[32,128]{1,0:T(8,128)}) custom-call(bf16[8,2,192,128]{3,2,1,0:T(8,128)(2,1)} %all-to-all-done.qkv_ref, bf16[2,1024,1024]{2,1,0:T(8,128)(2,1)} %get-tuple-element.109.weight_ref, f32[2,64,1024]{2,1,0:T(8,128)} %get-tuple-element.110.att_ref, f32[2,1,1024]{2,1,0:T(1,128)} %get-tuple-element.111.total_ref, ...), custom_call_target="tpu_custom_call" | custom-call | bytes 42000000 | tf_op jit(solution)/shard_map/attend_back/pallas_call | solution.py:338
  88.4 4.4 %all-to-all-start.3 = ((bf16[8,2,192,128]{3,2,1,0:T(8,128)(2,1)}), bf16[8,2,192,128]{3,2,1,0:T(8,128)(2,1)}, u32[]{:S(2)}, u32[]{:S(2)}) async-start(bf16[8,2,192,128]{3,2,1,0:T(8,128)(2,1)} %get-tuple-element.119), calls=%async_computation.3 | async-start | bytes 1572864 | tf_op jit(solution)/shard_map/all_to_all | solution.py:984
  92.7 4.0 %collective-permute-done.4.refs_1_ = bf16[2,4,32,1536]{3,2,1,0:T(8,128)(2,1)} collective-permute-done((bf16[2,4,32,1536]{3,2,1,0:T(8,128)(2,1)}, bf16[2,4,32,1536]{3,2,1,0:T(8,128)(2,1)}, u32[]{:S(2)}, u32[]{:S(2)}) %collective-permute-start.4) | collective-permute-done | bytes 786464 | tf_op jit(solution)/shard_map/ppermute | solution.py:917
  100.0 3.8 %collective-permute-done.6.refs_4_ = bf16[2,4,32,1536]{3,2,1,0:T(8,128)(2,1)} collective-permute-done((bf16[2,4,32,1536]{3,2,1,0:T(8,128)(2,1)}, bf16[2,4,32,1536]{3,2,1,0:T(8,128)(2,1)}, u32[]{:S(2)}, u32[]{:S(2)}) %collective-permute-start.6) | collective-permute-done | bytes 786464 | tf_op jit(solution)/shard_map/ppermute | solution.py:917
  106.2 6.4 %all-to-all-done.3.refs_0_ = bf16[8,2,192,128]{3,2,1,0:T(8,128)(2,1)} async-done(((bf16[8,2,192,128]{3,2,1,0:T(8,128)(2,1)}), bf16[8,2,192,128]{3,2,1,0:T(8,128)(2,1)}, u32[]{:S(2)}, u32[]{:S(2)}) %all-to-all-start.3) | async-done | bytes 786464 | tf_op jit(solution)/shard_map/all_to_all | solution.py:984
  112.6 6.4 %last.1 = (bf16[4,4,16,2688]{3,2,1,0:T(8,128)(2,1)}, bf16[4,4,16,2688]{3,2,1,0:T(8,128)(2,1)}, f32[2,128,512]{2,1,0:T(8,128)}, f32[2,8,512]{2,1,0:T(8,128)}) custom-call(bf16[8,2,192,128]{3,2,1,0:T(8,128)(2,1)} %all-to-all-done.3.refs_0_, bf16[256,512]{1,0:T(8,128)(2,1)} %get-tuple-element.120.refs_1_, bf16[512,512]{1,0:T(8,128)(2,1)} %refs_2_.5, ...), custom_call_target="tpu_custom_call" | custom-call | bytes 24500000 | tf_op jit(solution)/shard_map/last/pallas_call | solution.py:705
  133.8 6.5 %collective-permute-done.10 = bf16[32,3072]{1,0:T(8,128)(2,1)S(1)} collective-permute-done((bf16[32,3072]{1,0:T(8,128)(2,1)}, bf16[32,3072]{1,0:T(8,128)(2,1)S(1)}, u32[]{:S(2)}, u32[]{:S(2)}) %collective-permute-start.10) | collective-permute-done | bytes 196640 | tf_op jit(solution)/shard_map/ppermute | solution.py:917
  141.5 6.4 %collective-permute-start.13 = (bf16[32,3072]{1,0:T(8,128)(2,1)S(1)}, bf16[32,3072]{1,0:T(8,128)(2,1)S(1)}, u32[]{:S(2)}, u32[]{:S(2)}) collective-permute-start(bf16[32,3072]{1,0:T(8,128)(2,1)S(1)} %add_convert_fusion.3.refs_0_), channel_id=1, source_target_pairs={{0,16},{4,20},{8,24},{12,28},{16,0},{20,4},{24,8},{28,12},{1,17},{... | collective-permute-start | bytes 589832 | tf_op jit(solution)/shard_map/ppermute | solution.py:917
  149.4 10.8 %collective-permute-done.13.refs_2_ = bf16[32,3072]{1,0:T(8,128)(2,1)S(1)} collective-permute-done((bf16[32,3072]{1,0:T(8,128)(2,1)S(1)}, bf16[32,3072]{1,0:T(8,128)(2,1)S(1)}, u32[]{:S(2)}, u32[]{:S(2)}) %collective-permute-start.13) | collective-permute-done | bytes 196640 | tf_op jit(solution)/shard_map/ppermute | solution.py:917
  161.9 4.2 %all-to-all-start.5 = ((bf16[4,16,2688]{2,1,0:T(8,128)(2,1)}), bf16[4,16,2688]{2,1,0:T(8,128)(2,1)}, u32[]{:S(2)}, u32[]{:S(2)}) async-start(bf16[4,16,2688]{2,1,0:T(8,128)(2,1)} %reduce.20), calls=%async_computation.5 | async-start | bytes 688128 | tf_op jit(solution)/shard_map/all_to_all | solution.py:955
  172.4 4.6 %all-to-all-done.5 = bf16[4,16,2688]{2,1,0:T(8,128)(2,1)} async-done(((bf16[4,16,2688]{2,1,0:T(8,128)(2,1)}), bf16[4,16,2688]{2,1,0:T(8,128)(2,1)}, u32[]{:S(2)}, u32[]{:S(2)}) %all-to-all-start.5) | async-done | bytes 344096 | tf_op jit(solution)/shard_map/all_to_all | solution.py:955
  182.3 5.7 %collective-permute-done.18.refs_2_ = bf16[4,32,1536]{2,1,0:T(8,128)(2,1)} collective-permute-done((bf16[4,32,1536]{2,1,0:T(8,128)(2,1)}, bf16[4,32,1536]{2,1,0:T(8,128)(2,1)}, u32[]{:S(2)}, u32[]{:S(2)}) %collective-permute-start.18) | collective-permute-done | bytes 393248 | tf_op jit(solution)/shard_map/ppermute | solution.py:917
  192.4 7.1 %collective-permute-done.21.spill_ref = f32[2,3,512]{2,1,0:T(4,128)S(1)} collective-permute-done((f32[2,3,512]{2,1,0:T(4,128)S(1)}, f32[2,3,512]{2,1,0:T(4,128)S(1)}, u32[]{:S(2)}, u32[]{:S(2)}) %collective-permute-start.21) | collective-permute-done | bytes 12320 | tf_op jit(solution)/shard_map/ppermute | solution.py:30
  200.8 4.4 %all-to-all-start.7 = ((bf16[4,4,16,2688]{3,2,1,0:T(8,128)(2,1)}), bf16[4,4,16,2688]{3,2,1,0:T(8,128)(2,1)}, u32[]{:S(2)}, u32[]{:S(2)}) async-start(bf16[4,4,16,2688]{3,2,1,0:T(8,128)(2,1)} %broadcast_in_dim.8), calls=%async_computation.7 | async-start | bytes 2752512 | tf_op jit(solution)/shard_map/all_to_all | solution.py:949
  210.8 4.2 %unplace_ffn.2 = (f32[512,2048]{1,0:T(8,128)}, f32[512,2048]{1,0:T(8,128)}, f32[2048,512]{1,0:T(8,128)}) custom-call(bf16[4,32,1536]{2,1,0:T(8,128)(2,1)} %get-tuple-element.161.refs_0_, bf16[4,32,1536]{2,1,0:T(8,128)(2,1)} %copy-done.5, bf16[4,32,1536]{2,1,0:T(8,128)(2,1)} %copy-done.4, bf16[4,32,1536]{2,1,0:T(8,128)(2,1)} %copy-done.6, ...), custom_call_target="tpu_custom_call" | custom-call | bytes 14000000 | tf_op jit(solution)/shard_map/unplace_ffn/pallas_call | solution.py:830
  215.1 4.2 %unplace_ffn.3 = (f32[512,2048]{1,0:T(8,128)}, f32[512,2048]{1,0:T(8,128)}, f32[2048,512]{1,0:T(8,128)}) custom-call(bf16[4,32,1536]{2,1,0:T(8,128)(2,1)} %get-tuple-element.157.refs_0_, bf16[4,32,1536]{2,1,0:T(8,128)(2,1)} %collective-permute-done.17.refs_1_, ...), custom_call_target="tpu_custom_call", output_to_operand_aliasing={{0}: (8, {}), {1}: (9, {}), {2}: (10, {})} | custom-call | bytes 14000000 | tf_op jit(solution)/shard_map/unplace_ffn/pallas_call | solution.py:830
  (114 shorter events, 70.0 us)
Async XLA Ops:
  11.9 25.8 %all-to-all-start = ((bf16[8,2,192,128]{3,2,1,0:T(8,128)(2,1)}), bf16[8,2,192,128]{3,2,1,0:T(8,128)(2,1)}, u32[]{:S(2)}, u32[]{:S(2)}) async-start(bf16[8,2,192,128]{3,2,1,0:T(8,128)(2,1)} %get-tuple-element.105), calls=%async_computation | async-start | bytes 1572864 | tf_op jit(solution)/shard_map/all_to_all | solution.py:984
  63.4 13.9 %all-to-all-start.2 = ((bf16[8,2,64,128]{3,2,1,0:T(8,128)(2,1)}), bf16[8,2,64,128]{3,2,1,0:T(8,128)(2,1)}, u32[]{:S(2)}, u32[]{:S(2)}) async-start(bf16[8,2,64,128]{3,2,1,0:T(8,128)(2,1)} %get-tuple-element.112), calls=%async_computation.2 | async-start | bytes 524288 | tf_op jit(solution)/shard_map/all_to_all | solution.py:984
  77.3 19.4 %collective-permute-start.4 = (bf16[2,4,32,1536]{3,2,1,0:T(8,128)(2,1)}, bf16[2,4,32,1536]{3,2,1,0:T(8,128)(2,1)}, u32[]{:S(2)}, u32[]{:S(2)}) collective-permute-start(bf16[2,4,32,1536]{3,2,1,0:T(8,128)(2,1)} %get-tuple-element.128), channel_id=1, source_target_pairs={{0,2},{1,3},{2,0},{3,1},{4,6},{5,7},{6,4},{7,5},{8,10},{9,11},{10,... | collective-permute-start | bytes 2359304 | tf_op jit(solution)/shard_map/ppermute | solution.py:917
  78.8 25.0 %collective-permute-start.6 = (bf16[2,4,32,1536]{3,2,1,0:T(8,128)(2,1)}, bf16[2,4,32,1536]{3,2,1,0:T(8,128)(2,1)}, u32[]{:S(2)}, u32[]{:S(2)}) collective-permute-start(bf16[2,4,32,1536]{3,2,1,0:T(8,128)(2,1)} %get-tuple-element.130), channel_id=1, source_target_pairs={{0,4},{4,0},{8,12},{12,8},{16,20},{20,16},{24,28},{28,24},{1,5},{5... | collective-permute-start | bytes 2359304 | tf_op jit(solution)/shard_map/ppermute | solution.py:917
  88.4 24.2 %all-to-all-start.3 = ((bf16[8,2,192,128]{3,2,1,0:T(8,128)(2,1)}), bf16[8,2,192,128]{3,2,1,0:T(8,128)(2,1)}, u32[]{:S(2)}, u32[]{:S(2)}) async-start(bf16[8,2,192,128]{3,2,1,0:T(8,128)(2,1)} %get-tuple-element.119), calls=%async_computation.3 | async-start | bytes 1572864 | tf_op jit(solution)/shard_map/all_to_all | solution.py:984
  98.5 20.4 %collective-permute-start.5 = (bf16[1,4,32,1536]{3,2,1,0:T(8,128)(2,1)}, bf16[1,4,32,1536]{3,2,1,0:T(8,128)(2,1)}, u32[]{:S(2)}, u32[]{:S(2)}) collective-permute-start(bf16[1,4,32,1536]{3,2,1,0:T(8,128)(2,1)} %add_convert_fusion.2), channel_id=1, source_target_pairs={{0,4},{4,0},{8,12},{12,8},{16,20},{20,16},{24,28},{28,24},{1,5},{5... | collective-permute-start | bytes 1179656 | tf_op jit(solution)/shard_map/ppermute | solution.py:917
  105.7 13.3 %collective-permute-start.7 = (bf16[1,4,32,1536]{3,2,1,0:T(8,128)(2,1)}, bf16[1,4,32,1536]{3,2,1,0:T(8,128)(2,1)}, u32[]{:S(2)}, u32[]{:S(2)}) collective-permute-start(bf16[1,4,32,1536]{3,2,1,0:T(8,128)(2,1)} %add_convert_fusion.1), channel_id=1, source_target_pairs={{0,2},{1,3},{2,0},{3,1},{4,6},{5,7},{6,4},{7,5},{8,10},{9,11},{10,... | collective-permute-start | bytes 1179656 | tf_op jit(solution)/shard_map/ppermute | solution.py:917
  122.5 11.2 %collective-permute-start.9 = (bf16[32,3072]{1,0:T(8,128)(2,1)}, bf16[32,3072]{1,0:T(8,128)(2,1)S(1)}, u32[]{:S(2)}, u32[]{:S(2)}) collective-permute-start(bf16[32,3072]{1,0:T(8,128)(2,1)} %get-tuple-element.140), channel_id=1, source_target_pairs={{0,8},{4,12},{8,0},{12,4},{16,24},{20,28},{24,16},{28,20},{1,9},{5... | collective-permute-start | bytes 589832 | tf_op jit(solution)/shard_map/ppermute | solution.py:917
  122.9 17.3 %collective-permute-start.10 = (bf16[32,3072]{1,0:T(8,128)(2,1)}, bf16[32,3072]{1,0:T(8,128)(2,1)S(1)}, u32[]{:S(2)}, u32[]{:S(2)}) collective-permute-start(bf16[32,3072]{1,0:T(8,128)(2,1)} %get-tuple-element.141), channel_id=1, source_target_pairs={{0,16},{4,20},{8,24},{12,28},{16,0},{20,4},{24,8},{28,12},{1,17},{... | collective-permute-start | bytes 589832 | tf_op jit(solution)/shard_map/ppermute | solution.py:917
  124.2 16.1 %collective-permute-start.11 = (bf16[32,3072]{1,0:T(8,128)(2,1)}, bf16[32,3072]{1,0:T(8,128)(2,1)S(1)}, u32[]{:S(2)}, u32[]{:S(2)}) collective-permute-start(bf16[32,3072]{1,0:T(8,128)(2,1)} %get-tuple-element.142), channel_id=1, source_target_pairs={{0,24},{4,28},{8,16},{12,20},{16,8},{20,12},{24,0},{28,4},{1,25},{... | collective-permute-start | bytes 589832 | tf_op jit(solution)/shard_map/ppermute | solution.py:917
  130.1 30.9 %all-to-all-start.4 = ((bf16[4,4,16,2688]{3,2,1,0:T(8,128)(2,1)}), bf16[4,4,16,2688]{3,2,1,0:T(8,128)(2,1)S(1)}, u32[]{:S(2)}, u32[]{:S(2)}) async-start(bf16[4,4,16,2688]{3,2,1,0:T(8,128)(2,1)} %add_convert_fusion), calls=%async_computation.4 | async-start | bytes 2752512 | tf_op jit(solution)/shard_map/all_to_all | solution.py:949
  140.4 9.0 %collective-permute-start.14 = (bf16[32,3072]{1,0:T(8,128)(2,1)S(1)}, bf16[32,3072]{1,0:T(8,128)(2,1)S(1)}, u32[]{:S(2)}, u32[]{:S(2)}) collective-permute-start(bf16[32,3072]{1,0:T(8,128)(2,1)S(1)} %add_convert_fusion.3.refs_0_), channel_id=1, source_target_pairs={{0,24},{4,28},{8,16},{12,20},{16,8},{20,12},{24,0},{28,4},{1,25},{... | collective-permute-start | bytes 589832 | tf_op jit(solution)/shard_map/ppermute | solution.py:917
  141.5 18.7 %collective-permute-start.13 = (bf16[32,3072]{1,0:T(8,128)(2,1)S(1)}, bf16[32,3072]{1,0:T(8,128)(2,1)S(1)}, u32[]{:S(2)}, u32[]{:S(2)}) collective-permute-start(bf16[32,3072]{1,0:T(8,128)(2,1)S(1)} %add_convert_fusion.3.refs_0_), channel_id=1, source_target_pairs={{0,16},{4,20},{8,24},{12,28},{16,0},{20,4},{24,8},{28,12},{1,17},{... | collective-permute-start | bytes 589832 | tf_op jit(solution)/shard_map/ppermute | solution.py:917
  147.9 13.0 %collective-permute-start.12 = (bf16[32,3072]{1,0:T(8,128)(2,1)S(1)}, bf16[32,3072]{1,0:T(8,128)(2,1)}, u32[]{:S(2)}, u32[]{:S(2)}) collective-permute-start(bf16[32,3072]{1,0:T(8,128)(2,1)S(1)} %add_convert_fusion.3.refs_0_), channel_id=1, source_target_pairs={{0,8},{4,12},{8,0},{12,4},{16,24},{20,28},{24,16},{28,20},{1,9},{5... | collective-permute-start | bytes 589832 | tf_op jit(solution)/shard_map/ppermute | solution.py:917
  161.9 15.0 %all-to-all-start.5 = ((bf16[4,16,2688]{2,1,0:T(8,128)(2,1)}), bf16[4,16,2688]{2,1,0:T(8,128)(2,1)}, u32[]{:S(2)}, u32[]{:S(2)}) async-start(bf16[4,16,2688]{2,1,0:T(8,128)(2,1)} %reduce.20), calls=%async_computation.5 | async-start | bytes 688128 | tf_op jit(solution)/shard_map/all_to_all | solution.py:955
  168.3 13.9 %collective-permute-start.16 = (bf16[4,32,1536]{2,1,0:T(8,128)(2,1)}, bf16[4,32,1536]{2,1,0:T(8,128)(2,1)S(1)}, u32[]{:S(2)}, u32[]{:S(2)}) collective-permute-start(bf16[4,32,1536]{2,1,0:T(8,128)(2,1)} %get-tuple-element.161.refs_0_), channel_id=1, source_target_pairs={{0,2},{1,3},{2,0},{3,1},{4,6},{5,7},{6,4},{7,5},{8,10},{9,11},{10,... | collective-permute-start | bytes 1179656 | tf_op jit(solution)/shard_map/ppermute | solution.py:917
  168.8 13.5 %collective-permute-start.15 = (bf16[4,32,1536]{2,1,0:T(8,128)(2,1)}, bf16[4,32,1536]{2,1,0:T(8,128)(2,1)S(1)}, u32[]{:S(2)}, u32[]{:S(2)}) collective-permute-start(bf16[4,32,1536]{2,1,0:T(8,128)(2,1)} %get-tuple-element.161.refs_0_), channel_id=1, source_target_pairs={{0,4},{4,0},{8,12},{12,8},{16,20},{20,16},{24,28},{28,24},{1,5},{5... | collective-permute-start | bytes 1179656 | tf_op jit(solution)/shard_map/ppermute | solution.py:917
  170.0 17.9 %collective-permute-start.18 = (bf16[4,32,1536]{2,1,0:T(8,128)(2,1)}, bf16[4,32,1536]{2,1,0:T(8,128)(2,1)}, u32[]{:S(2)}, u32[]{:S(2)}) collective-permute-start(bf16[4,32,1536]{2,1,0:T(8,128)(2,1)} %get-tuple-element.157.refs_0_), channel_id=1, source_target_pairs={{0,4},{4,0},{8,12},{12,8},{16,20},{20,16},{24,28},{28,24},{1,5},{5... | collective-permute-start | bytes 1179656 | tf_op jit(solution)/shard_map/ppermute | solution.py:917
  170.8 17.1 %collective-permute-start.17 = (bf16[4,32,1536]{2,1,0:T(8,128)(2,1)}, bf16[4,32,1536]{2,1,0:T(8,128)(2,1)}, u32[]{:S(2)}, u32[]{:S(2)}) collective-permute-start(bf16[4,32,1536]{2,1,0:T(8,128)(2,1)} %get-tuple-element.157.refs_0_), channel_id=1, source_target_pairs={{0,2},{1,3},{2,0},{3,1},{4,6},{5,7},{6,4},{7,5},{8,10},{9,11},{10,... | collective-permute-start | bytes 1179656 | tf_op jit(solution)/shard_map/ppermute | solution.py:917
  178.8 20.8 %all-to-all-start.6 = ((bf16[4,16,2688]{2,1,0:T(8,128)(2,1)}), bf16[4,16,2688]{2,1,0:T(8,128)(2,1)S(1)}, u32[]{:S(2)}, u32[]{:S(2)}) async-start(bf16[4,16,2688]{2,1,0:T(8,128)(2,1)} %broadcast_in_dim.7), calls=%async_computation.6 | async-start | bytes 688128 | tf_op jit(solution)/shard_map/all_to_all | solution.py:955
  187.9 11.6 %collective-permute-start.19 = (bf16[4,32,1536]{2,1,0:T(8,128)(2,1)S(1)}, bf16[4,32,1536]{2,1,0:T(8,128)(2,1)S(1)}, u32[]{:S(2)}, u32[]{:S(2)}) collective-permute-start(bf16[4,32,1536]{2,1,0:T(8,128)(2,1)S(1)} %collective-permute-done.15.refs_1_), channel_id=1, source_target_pairs={{0,2},{1,3},{2,0},{3,1},{4,6},{5,7},{6,4},{7,5},{8,10},{9,11},{10,... | collective-permute-start | bytes 1179656 | tf_op jit(solution)/shard_map/ppermute | solution.py:917
  189.5 10.0 %collective-permute-start.20 = (bf16[4,32,1536]{2,1,0:T(8,128)(2,1)}, bf16[4,32,1536]{2,1,0:T(8,128)(2,1)}, u32[]{:S(2)}, u32[]{:S(2)}) collective-permute-start(bf16[4,32,1536]{2,1,0:T(8,128)(2,1)} %collective-permute-done.17.refs_1_), channel_id=1, source_target_pairs={{0,4},{4,0},{8,12},{12,8},{16,20},{20,16},{24,28},{28,24},{1,5},{5... | collective-permute-start | bytes 1179656 | tf_op jit(solution)/shard_map/ppermute | solution.py:917
  200.8 19.9 %all-to-all-start.7 = ((bf16[4,4,16,2688]{3,2,1,0:T(8,128)(2,1)}), bf16[4,4,16,2688]{3,2,1,0:T(8,128)(2,1)}, u32[]{:S(2)}, u32[]{:S(2)}) async-start(bf16[4,4,16,2688]{3,2,1,0:T(8,128)(2,1)} %broadcast_in_dim.8), calls=%async_computation.7 | async-start | bytes 2752512 | tf_op jit(solution)/shard_map/all_to_all | solution.py:949
  205.9 9.2 %collective-permute-start.22 = (bf16[4,32,1536]{2,1,0:T(8,128)(2,1)}, bf16[4,32,1536]{2,1,0:T(8,128)(2,1)}, u32[]{:S(2)}, u32[]{:S(2)}) collective-permute-start(bf16[4,32,1536]{2,1,0:T(8,128)(2,1)} %get-tuple-element.157.refs_0_), channel_id=1, source_target_pairs={{0,1},{1,0},{2,3},{3,2},{4,5},{5,4},{6,7},{7,6},{8,9},{9,8},{10,11... | collective-permute-start | bytes 1179656 | tf_op jit(solution)/shard_map/ppermute | solution.py:917
  (31 other events, 241.6 us)
